TPU v7x, 512 devices: a whole 4x8x8 slice. The times are simulated.
512 devices in a mesh: island: 16 (over y, x_lo), fsdp: 32 (over x_hi, z, core).
Axes of the slice: x: 4 (x_hi: 2, x_lo: 2; x = x_hi * 2 + x_lo), y: 8, z: 8, core: 2. Of those that a mesh axis runs over, the one named last changes fastest.
Arguments:
- inner: bfloat16 [16, 1536, 3072], P('island', 'fsdp'), may hold values from -6 to 6
- outer: float32 [1536, 3072], P('fsdp'), may hold values from -6 to 6
- momentum: float32 [1536, 3072], P('fsdp'), may hold values from -4 to 4
- residual: float32 [16, 1536, 3072], P('island', 'fsdp'), may hold values from -4 to 4
Outputs:
- outer_next: float32 [1536, 3072], P('fsdp')
- momentum_next: float32 [1536, 3072], P('fsdp')
- residual_next: float32 [16, 1536, 3072], P('island', 'fsdp')
All inputs are finite; a program needn't handle non-finite values.
Results may differ from a plain program's by a relative error of at most 0.0003.
Values sent between devices are 32-bit elements; how exact they have to be, the bound alone decides.
A program may use at most 64 MiB of HBM per device.

v0:
```python
import math

import jax
import jax.numpy as jnp
from jax import lax
from jax.sharding import PartitionSpec as P

GROUP = 128
BAND = 32


outer_rate = 0.7
momentum_keep = 0.9


def cosine_low(group, band_width):
    freq = jnp.arange(group, dtype=jnp.float32)[:, None]
    place = jnp.arange(group, dtype=jnp.float32)[None, :]
    table = jnp.cos(math.pi * (2.0 * place + 1.0) * freq / (2.0 * group))
    scale = jnp.where(freq == 0, math.sqrt(1.0 / group), math.sqrt(2.0 / group))
    return (table * scale)[:band_width]


def per_device(inner, outer, momentum, residual):
    exact = lax.Precision.HIGHEST
    low = cosine_low(GROUP, BAND)
    group = GROUP
    band_width = BAND
    rows_dev, cols = outer.shape
    cblocks = cols // group
    acc = outer - inner[0].astype(jnp.float32) + residual[0]
    tall = lax.all_to_all(acc, "fsdp", split_axis=1, concat_axis=0, tiled=True)
    width = tall.shape[1]
    half = jnp.einsum("kn,rnc->rkc", low, tall.reshape(-1, group, width), precision=exact).reshape(
        -1, width
    )
    flat = lax.all_to_all(half, "fsdp", split_axis=0, concat_axis=1, tiled=True)
    band = jnp.einsum(
        "rbm,lm->rbl", flat.reshape(flat.shape[0], cblocks, group), low, precision=exact
    )
    total = lax.psum(band, "island")
    mean_band = total / lax.axis_size("island")
    paired = jnp.stack((band, mean_band))
    spread = jnp.einsum("srbl,lm->srbm", paired, low, precision=exact).reshape(
        2, paired.shape[1], cols
    )
    stacked = lax.all_to_all(spread, "fsdp", split_axis=2, concat_axis=1, tiled=True)
    width = stacked.shape[2]
    restored = jnp.einsum(
        "kn,srkc->srnc", low, stacked.reshape(2, -1, band_width, width), precision=exact
    )
    full = lax.all_to_all(
        restored.reshape(2, -1, width), "fsdp", split_axis=1, concat_axis=2, tiled=True
    )
    sent = full[0]
    update = full[1]
    residual_next = acc - sent
    momentum_next = momentum_keep * momentum + update
    outer_next = outer - outer_rate * (update + momentum_keep * momentum_next)
    return (outer_next, momentum_next, residual_next[None])


def solution(mesh):
    placed = (
        P("island", "fsdp", None),
        P("fsdp", None),
        P("fsdp", None),
        P("island", "fsdp", None),
    )
    return jax.shard_map(
        per_device,
        mesh=mesh,
        in_specs=placed,
        out_specs=(P("fsdp", None), P("fsdp", None), P("island", "fsdp", None)),
        check_vma=False,
    )
```

profile of v0, /device:TPU:1, one launch (start us, length us, event | category | flops | bytes accessed | tf_op | source)
XLA Modules:
  0.0 212.2 jit_solution(15042434903416553844)
XLA Ops:
  0.6 1.4 fusion
  2.0 0.3 all_to_all.46
  2.3 1.4 copy.40
  3.7 14.4 %all-to-all-start = ((f32[48,32,96]{2,0,1:T(8,128)}), f32[48,32,96]{2,0,1:T(8,128)S(1)}, u32[]{:S(2)}, u32[]{:S(2)}) async-start(f32[48,32,96]{2,0,1:T(8,128)} %copy.40), calls=%async_computation | async-start | bytes 1572864 | tf_op jit(solution)/shard_map/all_to_all | solution.py:32
  18.2 22.7 %all-to-all-done = f32[48,32,96]{2,0,1:T(8,128)S(1)} async-done(((f32[48,32,96]{2,0,1:T(8,128)}), f32[48,32,96]{2,0,1:T(8,128)S(1)}, u32[]{:S(2)}, u32[]{:S(2)}) %all-to-all-start) | async-done | bytes 589856 | tf_op jit(solution)/shard_map/all_to_all | solution.py:32
  40.9 0.6 convolution_bitcast_fusion.1
  41.5 18.8 %all_to_all.62 = f32[32,12,96]{2,1,0:T(8,128)S(1)} all-to-all(f32[32,12,96]{2,1,0:T(8,128)S(1)} %all_to_all.49), channel_id=1, replica_groups=mesh['island'=16,'fsdp'=32] {'fsdp'}, dimensions={0} | all-to-all | bytes 294912 | tf_op jit(solution)/shard_map/all_to_all | solution.py:37
  60.4 0.1 reshape.55
  60.5 0.3 fusion.10
  60.9 51.1 %psum.7 = f32[12,24,32]{2,1,0:T(8,128)S(1)} all-reduce(f32[12,24,32]{2,1,0:T(8,128)S(1)} %fusion.10), channel_id=1, replica_groups=mesh['island'=16,'fsdp'=32] {'island'}, use_global_device_ids=true, to_apply=%region_0.1 | all-reduce | flops 9216 | bytes 73728 | tf_op jit(solution)/shard_map/psum | solution.py:41
  112.1 0.4 fusion.2
  112.5 1.5 copy.57
  114.0 5.2 %reshape.62 = f32[32,1,2304]{2,1,0:T(1,128)S(1)} reshape(f32[3072,2,12]{2,1,0:T(2,128)S(1)} %bitcast.47) | data formatting | bytes 589824
  119.2 32.1 %all_to_all.63 = f32[32,1,2304]{2,1,0:T(1,128)S(1)} all-to-all(f32[32,1,2304]{2,1,0:T(1,128)S(1)} %reshape.62), channel_id=1, replica_groups=mesh['island'=16,'fsdp'=32] {'fsdp'}, dimensions={0} | all-to-all | bytes 589824 | tf_op jit(solution)/shard_map/all_to_all | solution.py:47
  151.3 0.5 broadcast.56
  151.8 1.3 reduce
  153.1 5.0 %reshape.63 = f32[3072,2,12]{2,1,0:T(2,128)S(1)} reshape(f32[32,2304]{1,0:T(8,128)S(1)} %reduce) | data formatting | bytes 589824
  158.2 1.4 copy.58
  159.6 0.3 copy.46
  159.9 2.0 convolution_bitcast_fusion
  161.9 0.9 copy.59
  162.9 44.8 %all_to_all.64 = f32[2,1536,96]{2,0,1:T(2,128)S(1)} all-to-all(f32[2,1536,96]{2,0,1:T(2,128)S(1)} %bitcast.49), channel_id=1, replica_groups=mesh['island'=16,'fsdp'=32] {'fsdp'}, dimensions={1} | all-to-all | bytes 2359296 | tf_op jit(solution)/shard_map/all_to_all | solution.py:52
  207.7 0.1 fusion.39
  207.9 0.3 copy.52
  208.1 0.4 squeeze.12
  208.5 0.4 copy-done.1
  208.9 0.9 subtract_bitcast_fusion
  209.8 0.3 copy.51
  210.1 0.4 squeeze.11
  210.5 0.4 copy-done.2
  210.9 0.2 copy-done.3
  211.0 1.1 multiply_subtract_fusion
  (11 shorter events, 0.2 us)
Async XLA Ops:
  2.0 1.7 copy-start
  3.7 37.2 %all-to-all-start = ((f32[48,32,96]{2,0,1:T(8,128)}), f32[48,32,96]{2,0,1:T(8,128)S(1)}, u32[]{:S(2)}, u32[]{:S(2)}) async-start(f32[48,32,96]{2,0,1:T(8,128)} %copy.40), calls=%async_computation | async-start | bytes 1572864 | tf_op jit(solution)/shard_map/all_to_all | solution.py:32
  207.9 1.1 copy-start.1
  209.8 1.1 copy-start.2
  209.8 1.2 copy-start.3
where the time goes:
time: 213 us; the launch traced here: 212 us
  blocking collectives  147 us (69%)
  waiting for transfers between devices  22.7 us (11%)
  local copies, waits for them, and re-layouts  19.2 us (9%)
  starting transfers between devices  14.4 us (7%)
  other arithmetic  4.79 us (2%)
  matrix products  3.44 us (2%)
    psum x1, blocking collectives, per_device(): total = lax.psum(band, 'island')  51.1 us
    all_to_all x1, blocking collectives, per_device(): lax.all_to_all(restored.reshape(2, -1, width), 'fsdp', split_axis=1, conc...  44.8 us
    all_to_all x1, blocking collectives, per_device(): lax.all_to_all(spread, 'fsdp', split_axis=2, concat_axis=1, tiled=True)  32.1 us
    all_to_all x1, waiting for transfers between devices, per_device(): tall = lax.all_to_all(acc, 'fsdp', split_axis=1, concat_axis=0, tiled=True)  22.7 us
    all_to_all x1, blocking collectives, per_device(): flat = lax.all_to_all(half, 'fsdp', split_axis=0, concat_axis=1, tiled=True)  18.8 us
    all_to_all x1, starting transfers between devices, per_device(): tall = lax.all_to_all(acc, 'fsdp', split_axis=1, concat_axis=0, tiled=True)  14.4 us
    unnamed x10, local copies, waits for them, and re-layouts  11.2 us
  transfers between devices with their start and end apart: 1, of which 1 were waited for; matrix products, arithmetic and copies ran while one was open for 0% of the time, Pallas kernels for 0%

commit v1 on v0

v1 whole, which is shorter than its diff:
```python
import functools

import jax
import jax.numpy as jnp
import ml_dtypes
import numpy as np
from jax import lax
from jax.experimental import pallas as pl
from jax.experimental.pallas import tpu as pltpu
from jax.sharding import PartitionSpec as P

GROUP = 128
BAND = 32
ROWS_DEV = 48
RING = 8
OUTER_RATE = 0.7
KEEP = 0.9
MESH = pl.DeviceIdType.MESH
BF16 = ml_dtypes.bfloat16


def split_np(a):
    hi = a.astype(np.float32).astype(BF16)
    lo = (a - hi.astype(np.float64)).astype(np.float32).astype(BF16)
    return hi, lo


def cosine_low():
    freq = np.arange(BAND, dtype=np.float64)[:, None]
    place = np.arange(GROUP, dtype=np.float64)[None, :]
    table = np.cos(np.pi * (2.0 * place + 1.0) * freq / (2.0 * GROUP))
    scale = np.where(freq == 0, np.sqrt(1.0 / GROUP), np.sqrt(2.0 / GROUP))
    return table * scale


def tables():
    low = cosine_low()
    diag = np.zeros((4 * GROUP, 4 * BAND))
    for q in range(4):
        diag[q * GROUP : (q + 1) * GROUP, q * BAND : (q + 1) * BAND] = low.T
    hi, lo = split_np(diag)
    col_fwd = np.concatenate([hi, lo], axis=1)
    hi, lo = split_np(diag.T)
    col_inv = np.concatenate([hi, hi, lo], axis=0)
    row_fwd = np.zeros((RING, 2 * BAND, 3 * ROWS_DEV), BF16)
    row_inv = np.zeros((RING, ROWS_DEV, 3 * 2 * BAND), BF16)
    for d in range(RING):
        rows = d * ROWS_DEV + np.arange(ROWS_DEV)
        first, last = rows[0] // GROUP, rows[-1] // GROUP
        part = np.zeros((2 * BAND, ROWS_DEV))
        for slot, b in enumerate((first, last)):
            if slot == 1 and first == last:
                continue
            inside = rows // GROUP == b
            part[slot * BAND : (slot + 1) * BAND, inside] = low[:, rows[inside] % GROUP]
        hi, lo = split_np(part)
        row_fwd[d] = np.concatenate([hi, hi, lo], axis=1)
        hi, lo = split_np(part.T)
        row_inv[d] = np.concatenate([hi, hi, lo], axis=1)
    return col_fwd, col_inv, row_fwd, row_inv


def split(a):
    hi = a.astype(jnp.bfloat16)
    lo = (a - hi.astype(jnp.float32)).astype(jnp.bfloat16)
    return hi, lo


def dot(a, b):
    return jnp.dot(a, b, preferred_element_type=jnp.float32)


def kernel(
    ny, cols,
    inner_in, outer_in, mom_in, res_in, colf_in, coli_in, rowf_in, rowi_in,
    outer_out, mom_out, res_out,
    inner_v, outer_v, mom_v, res_v, colf, coli, rowf, rowi,
    part, from_a, sums, from_y, band, total, load_sem, out_sem,
    a_send, a_recv, y_send, y_recv, b_send, b_recv, t_send, t_recv,
):
    hc = cols * BAND // GROUP // 2
    i, f = lax.axis_index("island"), lax.axis_index("fsdp")
    y, xl = lax.div(i, 2), lax.rem(i, 2)
    d = lax.rem(f, RING)
    base = f - d
    lo_b, hi_b = lax.div(3 * d, 8), lax.div(3 * d + 2, 8)
    first = lambda b: lax.div(8 * b, 3)
    last = lambda b: lax.div(8 * b + 7, 3)
    own_b, half = lax.div(d, 3), lax.rem(d, 3)
    owner = half != 2
    two = lo_b != hi_b

    def at(yy, xx, dd):
        return (yy * 2 + xx, base + dd)

    bar = pltpu.get_barrier_semaphore()
    lo_d, hi_d = first(lo_b), last(hi_b)
    for k in range(-3, 4):
        for xr in range(2):
            if k == 0 and xr == 0:
                continue

            @pl.when((d + k >= lo_d) & (d + k <= hi_d))
            def _():
                pl.semaphore_signal(bar, 1, device_id=at(y, lax.rem(xl + xr, 2), d + k), device_id_type=MESH)

    for k in range(1, ny):
        pl.semaphore_signal(bar, 1, device_id=at(lax.rem(y + k, ny), xl, d), device_id_type=MESH)

    loads = [
        pltpu.make_async_copy(src, dst, load_sem.at[n])
        for n, (src, dst) in enumerate(
            [
                (inner_in.at[0], inner_v), (res_in.at[0], res_v), (outer_in, outer_v), (colf_in, colf), (rowf_in.at[d], rowf),
                (coli_in, coli), (rowi_in.at[d], rowi), (mom_in, mom_v),
            ]
        )
    ]
    for c in loads:
        c.start()

    @pl.when(own_b != 1)
    def _():
        from_a[6:8] = jnp.zeros((2, 16, hc), jnp.float32)

    @pl.when(jnp.logical_not(two))
    def _():
        band[BAND:] = jnp.zeros((BAND, 2 * hc), jnp.float32)
        total[BAND:] = jnp.zeros((BAND, 2 * hc), jnp.float32)

    for c in loads[:5]:
        c.wait()

    res_v[...] = outer_v[...] - inner_v[...].astype(jnp.float32) + res_v[...]
    chunks = cols // 512
    acc = jnp.concatenate([res_v[:, 512 * c : 512 * (c + 1)] for c in range(chunks)], axis=0)
    hi, lo = split(acc)
    prod = dot(hi, colf[...])
    tall = prod[:, :128] + prod[:, 128:] + dot(lo, colf[:, :128])
    wide = jnp.concatenate([tall[ROWS_DEV * c : ROWS_DEV * (c + 1)] for c in range(chunks)], axis=1)
    hi, lo = split(wide)
    part[...] = dot(rowf[...], jnp.concatenate([hi, lo, hi], axis=0))

    pl.semaphore_wait(bar, (hi_d - lo_d + 1) * 2 - 1 + ny - 1)

    def rows16(n):
        return pl.ds(pl.multiple_of(n * 16, 16), 16)

    def half_cols(xx):
        return pl.ds(pl.multiple_of(xx * hc, 128), hc)

    def a_copies(run):
        for slot, b in enumerate((lo_b, hi_b)):
            for h in range(2):
                for xr in range(2):
                    to_x = lax.rem(xl + xr, 2)
                    to_d = 3 * b + h
                    cond = jnp.logical_not((to_d == d) & (xr == 0)) if slot == 0 else two
                    n = slot * 4 + h * 2 + xr

                    @pl.when(cond)
                    def _():
                        run(
                            pltpu.make_async_remote_copy(
                                part.at[slot * BAND + 16 * h : slot * BAND + 16 * h + 16, half_cols(to_x)],
                                from_a.at[(d - first(b)) * 2 + xl],
                                a_send.at[n],
                                a_recv.at[(d - first(b)) * 2 + xl],
                                device_id=at(y, to_x, to_d),
                                device_id_type=MESH,
                            )
                        )

    a_copies(lambda c: c.start())

    me_a = (d - first(own_b)) * 2 + xl

    @pl.when(owner)
    def _():
        from_a[me_a] = part[rows16(half), half_cols(xl)]

    def dummy(ref, send, recv):
        return pltpu.make_async_remote_copy(ref, ref, send, recv, device_id=at(y, 1 - xl, d), device_id_type=MESH)

    @pl.when(owner)
    def _():
        for n in range(8):
            @pl.when((n != me_a) & (first(own_b) + n // 2 <= last(own_b)))
            def _():
                dummy(from_a.at[n], a_send.at[n], a_recv.at[n]).wait_recv()

        def add(x):
            return (from_a[x] + from_a[2 + x]) + (from_a[4 + x] + from_a[6 + x])

        mine, other = add(xl), add(1 - xl)
        sums[0] = mine
        sums[1] = other
        from_y[y] = mine + other

    def y_copies(run):
        for k in range(1, ny):
            run(
                pltpu.make_async_remote_copy(
                    from_y.at[y], from_y.at[y], y_send.at[k], y_recv.at[y],
                    device_id=at(lax.rem(y + k, ny), xl, d), device_id_type=MESH,
                )
            )

    def b_copies(run, src, dst, send, recv):
        for m in range(4):
            to_d = first(own_b) + m
            slot = own_b - lax.div(3 * to_d, 8)
            for xr in range(2):
                @pl.when((to_d <= last(own_b)) & jnp.logical_not((to_d == d) & (xr == 0)))
                def _():
                    run(
                        pltpu.make_async_remote_copy(
                            src(xr),
                            dst.at[rows16(slot * 2 + half), half_cols(xl)],
                            send.at[m * 2 + xr],
                            recv.at[slot * 4 + half * 2 + xl],
                            device_id=at(y, lax.rem(xl + xr, 2), to_d),
                            device_id_type=MESH,
                        )
                    )

    def b_wait(dst, send, recv):
        for slot in range(2):
            for h in range(2):
                for x in range(2):
                    n = slot * 4 + h * 2 + x
                    cond = two if slot == 1 else jnp.logical_not((3 * lo_b + h == d) & (x == xl))

                    @pl.when(cond)
                    def _():
                        dummy(
                            dst.at[slot * BAND + 16 * h : slot * BAND + 16 * h + 16, hc * x : hc * x + hc], send.at[n], recv.at[n]
                        ).wait_recv()

    @pl.when(owner)
    def _():
        y_copies(lambda c: c.start())
        b_copies(lambda c: c.start(), lambda xr: sums.at[xr], band, b_send, b_recv)
        band[rows16(half), half_cols(xl)] = sums[0]

    for c in loads[5:]:
        c.wait()

    def invert(coef):
        hi, lo = split(coef)
        wide = dot(rowi[...], jnp.concatenate([hi, lo, hi], axis=0))
        tall = jnp.concatenate([wide[:, 128 * c : 128 * (c + 1)] for c in range(chunks)], axis=0)
        hi, lo = split(tall)
        return dot(jnp.concatenate([hi, lo, hi], axis=1), coli[...])

    b_wait(band, b_send, b_recv)
    sent = invert(band[...])
    for c in range(chunks):
        at_c = slice(512 * c, 512 * (c + 1))
        res_v[:, at_c] = res_v[:, at_c] - sent[ROWS_DEV * c : ROWS_DEV * (c + 1)]
    res_write = pltpu.make_async_copy(res_v, res_out.at[0], out_sem.at[0])
    res_write.start()

    @pl.when(owner)
    def _():
        for k in range(1, ny):
            n = lax.rem(y + k, ny)
            dummy(from_y.at[n], y_send.at[k], y_recv.at[n]).wait_recv()
        whole = from_y[0]
        for n in range(1, ny):
            whole = whole + from_y[n]
        sums[2] = whole * (1.0 / (2 * ny))
        b_copies(lambda c: c.start(), lambda xr: sums.at[2], total, t_send, t_recv)
        total[rows16(half), half_cols(xl)] = sums[2]

    b_wait(total, t_send, t_recv)
    update = invert(total[...])
    for c in range(chunks):
        at_c = slice(512 * c, 512 * (c + 1))
        u = update[ROWS_DEV * c : ROWS_DEV * (c + 1)]
        m = KEEP * mom_v[:, at_c] + u
        mom_v[:, at_c] = m
        outer_v[:, at_c] = outer_v[:, at_c] - OUTER_RATE * (u + KEEP * m)
    writes = [
        pltpu.make_async_copy(mom_v, mom_out, out_sem.at[1]),
        pltpu.make_async_copy(outer_v, outer_out, out_sem.at[2]),
    ]
    for c in writes:
        c.start()
    a_copies(lambda c: c.wait_send())

    @pl.when(owner)
    def _():
        y_copies(lambda c: c.wait_send())
        b_copies(lambda c: c.wait_send(), lambda xr: sums.at[xr], band, b_send, b_recv)
        b_copies(lambda c: c.wait_send(), lambda xr: sums.at[2], total, t_send, t_recv)

    res_write.wait()
    for c in writes:
        c.wait()


def solution(mesh):
    ny = mesh.shape["island"] // 2
    col_fwd, col_inv, row_fwd, row_inv = tables()

    def per_device(inner, outer, momentum, residual):
        rows, cols = outer.shape
        hc = cols * BAND // GROUP // 2
        f32, bf16 = jnp.float32, jnp.bfloat16
        dma = pltpu.SemaphoreType.DMA
        return tuple(
            pl.pallas_call(
                functools.partial(kernel, ny, cols),
                name="outer_step",
                out_shape=[
                    jax.ShapeDtypeStruct((rows, cols), f32),
                    jax.ShapeDtypeStruct((rows, cols), f32),
                    jax.ShapeDtypeStruct((1, rows, cols), f32),
                ],
                in_specs=[pl.BlockSpec(memory_space=pltpu.HBM)] * 8,
                out_specs=[pl.BlockSpec(memory_space=pl.ANY)] * 3,
                scratch_shapes=[
                    pltpu.VMEM((rows, cols), bf16),
                    pltpu.VMEM((rows, cols), f32),
                    pltpu.VMEM((rows, cols), f32),
                    pltpu.VMEM((rows, cols), f32),
                    pltpu.VMEM(col_fwd.shape, bf16),
                    pltpu.VMEM(col_inv.shape, bf16),
                    pltpu.VMEM(row_fwd.shape[1:], bf16),
                    pltpu.VMEM(row_inv.shape[1:], bf16),
                    pltpu.VMEM((2 * BAND, 2 * hc), f32),
                    pltpu.VMEM((8, 16, hc), f32),
                    pltpu.VMEM((3, 16, hc), f32),
                    pltpu.VMEM((ny, 16, hc), f32),
                    pltpu.VMEM((2 * BAND, 2 * hc), f32),
                    pltpu.VMEM((2 * BAND, 2 * hc), f32),
                    dma((8,)), dma((3,)),
                    dma((8,)), dma((8,)), dma((ny,)), dma((ny,)), dma((8,)), dma((8,)), dma((8,)), dma((8,)),
                ],
                compiler_params=pltpu.CompilerParams(
                    collective_id=0, has_side_effects=True, vmem_limit_bytes=40 * 1024 * 1024
                ),
            )(
                inner, outer, momentum, residual,
                jnp.asarray(col_fwd), jnp.asarray(col_inv), jnp.asarray(row_fwd), jnp.asarray(row_inv),
            )
        )

    return jax.shard_map(
        per_device,
        mesh=mesh,
        in_specs=(P("island", "fsdp", None), P("fsdp", None), P("fsdp", None), P("island", "fsdp", None)),
        out_specs=(P("fsdp", None), P("fsdp", None), P("island", "fsdp", None)),
        check_vma=False,
    )
```

time: 213 us -> 37.4 us (0.18)
  blocking collectives: 147 us -> 0 us
  Pallas kernels: 0 us -> 25.9 us
  waiting for transfers between devices: 22.7 us -> 0 us
  starting transfers between devices: 14.4 us -> 0 us
  local copies, waits for them, and re-layouts: 19.2 us -> 10.4 us
  other arithmetic: 4.79 us -> 0 us
  matrix products: 3.44 us -> 0 us
    all_to_all x3 -> x0, blocking collectives: 95.7 us -> none  [the longest x1 44.8 us: per_device(): lax.all_to_all(restored.reshape(2, -1, width), 'fsdp', split_axis=1, conc...]
    psum x1 -> x0, blocking collectives: 51.1 us -> none  [per_device(): total = lax.psum(band, 'island')]
    pallas_call x0 -> x1, Pallas kernels: none -> 25.9 us  [per_device(): pl.pallas_call(functools.partial(kernel, ny, cols), name='outer_step', ou...]
    all_to_all x1 -> x0, waiting for transfers between devices: 22.7 us -> none  [per_device(): tall = lax.all_to_all(acc, 'fsdp', split_axis=1, concat_axis=0, tiled=True)]
    all_to_all x1 -> x0, starting transfers between devices: 14.4 us -> none  [per_device(): tall = lax.all_to_all(acc, 'fsdp', split_axis=1, concat_axis=0, tiled=True)]
    all_to_all x8 -> x0, local copies, waits for them, and re-layouts: 4.04 us -> none  [the longest x3 2.21 us: per_device(): lax.all_to_all(spread, 'fsdp', split_axis=2, concat_axis=1, tiled=True)]
    dot_general x4 -> x0, matrix products: 3.44 us -> none  [the longest x1 2.04 us: per_device(): jnp.einsum('kn,srkc->srnc', low, stacked.reshape(2, -1, band_width, width...]
    reshape x3 -> x0, local copies, waits for them, and re-layouts: 2.51 us -> none  [the longest x1 1.46 us: per_device(): jnp.einsum('srbl,lm->srbm', paired, low, precision=exact)]
  transfers between devices with their start and end apart: 1 -> 0, of which waited for: 1 -> 0; matrix products, arithmetic and copies ran while one was open for 0% -> 0% of each run, Pallas kernels for 0% -> 0%
where the time goes in v1:
time: 37.4 us; the launch traced here: 36.9 us
  Pallas kernels  25.9 us (69%)
  local copies, waits for them, and re-layouts  10.4 us (28%)
  between operations  0.66 us (2%)
    pallas_call x1, Pallas kernels, per_device(): pl.pallas_call(functools.partial(kernel, ny, cols), name='outer_step', ou...  25.9 us
    unnamed x19, local copies, waits for them, and re-layouts  10.4 us

profile of v1, /device:TPU:1, one launch (start us, length us, event | category | flops | bytes accessed | tf_op | source)
XLA Modules:
  0.0 36.9 jit_solution(3419590875585794104)
XLA Ops:
  0.6 0.0 copy-start
  0.6 1.1 %copy-done = f32[48,3072]{1,0:T(8,128)S(1)} copy-done((f32[48,3072]{1,0:T(8,128)S(1)}, f32[48,3072]{1,0:T(8,128)}, u32[]{:S(2)}) %copy-start) | copy-done | bytes 589848
  1.7 0.0 copy-start.1
  1.7 1.1 %copy-done.1 = f32[48,3072]{1,0:T(8,128)S(1)} copy-done((f32[48,3072]{1,0:T(8,128)S(1)}, f32[48,3072]{1,0:T(8,128)}, u32[]{:S(2)}) %copy-start.1) | copy-done | bytes 589848
  2.8 0.0 copy-start.2
  2.8 1.1 %copy-done.2 = f32[1,48,3072]{2,1,0:T(8,128)S(1)} copy-done((f32[1,48,3072]{2,1,0:T(8,128)S(1)}, f32[1,48,3072]{2,1,0:T(8,128)}, u32[]{:S(2)}) %copy-start.2) | copy-done | bytes 589848
  3.8 0.0 copy-start.3
  3.8 1.0 %copy-done.3 = bf16[384,512]{1,0:T(8,128)(2,1)S(1)} copy-done((bf16[384,512]{1,0:T(8,128)(2,1)S(1)}, bf16[384,512]{1,0:T(8,128)(2,1)}, u32[]{:S(2)}) %copy-start.3) | copy-done | bytes 393240
  4.8 0.0 copy-start.4
  4.8 1.0 %copy-done.4 = bf16[1,48,3072]{2,1,0:T(8,128)(2,1)S(1)} copy-done((bf16[1,48,3072]{2,1,0:T(8,128)(2,1)S(1)}, bf16[1,48,3072]{2,1,0:T(8,128)(2,1)}, u32[]{:S(2)}) %copy-start.4) | copy-done | bytes 294936
  5.8 0.0 copy-start.5
  5.8 0.9 %copy-done.5 = bf16[8,64,144]{2,1,0:T(8,128)(2,1)S(1)} copy-done((bf16[8,64,144]{2,1,0:T(8,128)(2,1)S(1)}, bf16[8,64,144]{2,1,0:T(8,128)(2,1)}, u32[]{:S(2)}) %copy-start.5) | copy-done | bytes 147480
  6.7 0.0 copy-start.6
  6.7 0.9 %copy-done.6 = bf16[512,256]{1,0:T(8,128)(2,1)S(1)} copy-done((bf16[512,256]{1,0:T(8,128)(2,1)S(1)}, bf16[512,256]{1,0:T(8,128)(2,1)}, u32[]{:S(2)}) %copy-start.6) | copy-done | bytes 262168
  7.7 0.0 copy-start.7
  7.7 0.9 %copy-done.7 = bf16[8,48,192]{2,1,0:T(8,128)(2,1)S(1)} copy-done((bf16[8,48,192]{2,1,0:T(8,128)(2,1)S(1)}, bf16[8,48,192]{2,1,0:T(8,128)(2,1)}, u32[]{:S(2)}) %copy-start.7) | copy-done | bytes 147480
  8.6 25.9 %outer_step.1 = (f32[48,3072]{1,0:T(8,128)S(1)}, f32[48,3072]{1,0:T(8,128)S(1)}, f32[1,48,3072]{2,1,0:T(8,128)S(1)}) custom-call(bf16[1,48,3072]{2,1,0:T(8,128)(2,1)S(1)} %copy-done.4, f32[48,3072]{1,0:T(8,128)S(1)} %copy-done, f32[48,3072]{1,0:T(8,128)S(1)} %copy-done.1, f32[1,48,3072]{2,1,0:T(8,128)S(1)} %copy-done.2, bf16[512,256]{1,0:T(8,128)(2,1)S(1)} %copy-done.6, ...), custom_call_target="tpu_custom_call" | custom-call | tf_op jit(solution)/shard_map/outer_step/pallas_call | solution.py:313
  34.5 0.8 %copy.14 = f32[48,3072]{1,0:T(8,128)} copy(f32[48,3072]{1,0:T(8,128)S(1)} %get-tuple-element.6) | data formatting | bytes 1179648
  35.3 0.8 %copy.15 = f32[48,3072]{1,0:T(8,128)} copy(f32[48,3072]{1,0:T(8,128)S(1)} %get-tuple-element.7) | data formatting | bytes 1179648
  36.1 0.8 %copy.16 = f32[1,48,3072]{2,1,0:T(8,128)} copy(f32[1,48,3072]{2,1,0:T(8,128)S(1)} %get-tuple-element.8) | data formatting | bytes 1179648
Async XLA Ops:
  0.6 1.1 %copy-start = (f32[48,3072]{1,0:T(8,128)S(1)}, f32[48,3072]{1,0:T(8,128)}, u32[]{:S(2)}) copy-start(f32[48,3072]{1,0:T(8,128)} %outer_in.1) | copy-start | bytes 1769476
  1.7 1.1 %copy-start.1 = (f32[48,3072]{1,0:T(8,128)S(1)}, f32[48,3072]{1,0:T(8,128)}, u32[]{:S(2)}) copy-start(f32[48,3072]{1,0:T(8,128)} %mom_in.1) | copy-start | bytes 1769476
  2.8 1.1 %copy-start.2 = (f32[1,48,3072]{2,1,0:T(8,128)S(1)}, f32[1,48,3072]{2,1,0:T(8,128)}, u32[]{:S(2)}) copy-start(f32[1,48,3072]{2,1,0:T(8,128)} %res_in.1) | copy-start | bytes 1769476
  3.8 1.0 %copy-start.3 = (bf16[384,512]{1,0:T(8,128)(2,1)S(1)}, bf16[384,512]{1,0:T(8,128)(2,1)}, u32[]{:S(2)}) copy-start(bf16[384,512]{1,0:T(8,128)(2,1)} %constant.9.clone.coli_in) | copy-start | bytes 1179652
  4.8 1.0 %copy-start.4 = (bf16[1,48,3072]{2,1,0:T(8,128)(2,1)S(1)}, bf16[1,48,3072]{2,1,0:T(8,128)(2,1)}, u32[]{:S(2)}) copy-start(bf16[1,48,3072]{2,1,0:T(8,128)(2,1)} %inner_in.1) | copy-start | bytes 884740
  5.8 0.9 %copy-start.5 = (bf16[8,64,144]{2,1,0:T(8,128)(2,1)S(1)}, bf16[8,64,144]{2,1,0:T(8,128)(2,1)}, u32[]{:S(2)}) copy-start(bf16[8,64,144]{2,1,0:T(8,128)(2,1)} %constant.10.clone.rowf_in) | copy-start | bytes 442372
  6.7 0.9 %copy-start.6 = (bf16[512,256]{1,0:T(8,128)(2,1)S(1)}, bf16[512,256]{1,0:T(8,128)(2,1)}, u32[]{:S(2)}) copy-start(bf16[512,256]{1,0:T(8,128)(2,1)} %constant.8.clone.colf_in) | copy-start | bytes 786436
  7.7 0.9 %copy-start.7 = (bf16[8,48,192]{2,1,0:T(8,128)(2,1)S(1)}, bf16[8,48,192]{2,1,0:T(8,128)(2,1)}, u32[]{:S(2)}) copy-start(bf16[8,48,192]{2,1,0:T(8,128)(2,1)} %constant.11.clone.rowi_in) | copy-start | bytes 442372

commit v2 on v1

--- a/solution.py
+++ b/solution.py
@@ -70,12 +70,20 @@
     return jnp.dot(a, b, preferred_element_type=jnp.float32)
 
 
+def invert(coef, rowi, coli):
+    hi, lo = split(coef)
+    wide = dot(rowi, jnp.concatenate([hi, lo, hi], axis=0))
+    tall = jnp.concatenate([wide[:, 128 * c : 128 * (c + 1)] for c in range(wide.shape[1] // 128)], axis=0)
+    hi, lo = split(tall)
+    return dot(jnp.concatenate([hi, lo, hi], axis=1), coli)
+
+
 def kernel(
     ny, cols,
-    inner_in, outer_in, mom_in, res_in, colf_in, coli_in, rowf_in, rowi_in,
-    outer_out, mom_out, res_out,
-    inner_v, outer_v, mom_v, res_v, colf, coli, rowf, rowi,
-    part, from_a, sums, from_y, band, total, load_sem, out_sem,
+    inner_in, outer_in, res_in, colf_in, coli_in, rowf_in, rowi_in,
+    total, res_out,
+    inner_v, outer_v, res_v, colf, coli, rowf, rowi,
+    part, from_a, sums, from_y, band, load_sem, out_sem,
     a_send, a_recv, y_send, y_recv, b_send, b_recv, t_send, t_recv,
 ):
     hc = cols * BAND // GROUP // 2
@@ -112,7 +120,7 @@
         for n, (src, dst) in enumerate(
             [
                 (inner_in.at[0], inner_v), (res_in.at[0], res_v), (outer_in, outer_v), (colf_in, colf), (rowf_in.at[d], rowf),
-                (coli_in, coli), (rowi_in.at[d], rowi), (mom_in, mom_v),
+                (coli_in, coli), (rowi_in.at[d], rowi),
             ]
         )
     ]
@@ -126,7 +134,6 @@
     @pl.when(jnp.logical_not(two))
     def _():
         band[BAND:] = jnp.zeros((BAND, 2 * hc), jnp.float32)
-        total[BAND:] = jnp.zeros((BAND, 2 * hc), jnp.float32)
 
     for c in loads[:5]:
         c.wait()
@@ -246,19 +253,12 @@
     for c in loads[5:]:
         c.wait()
 
-    def invert(coef):
-        hi, lo = split(coef)
-        wide = dot(rowi[...], jnp.concatenate([hi, lo, hi], axis=0))
-        tall = jnp.concatenate([wide[:, 128 * c : 128 * (c + 1)] for c in range(chunks)], axis=0)
-        hi, lo = split(tall)
-        return dot(jnp.concatenate([hi, lo, hi], axis=1), coli[...])
-
     b_wait(band, b_send, b_recv)
-    sent = invert(band[...])
+    sent = invert(band[...], rowi[...], coli[...])
     for c in range(chunks):
         at_c = slice(512 * c, 512 * (c + 1))
         res_v[:, at_c] = res_v[:, at_c] - sent[ROWS_DEV * c : ROWS_DEV * (c + 1)]
-    res_write = pltpu.make_async_copy(res_v, res_out.at[0], out_sem.at[0])
+    res_write = pltpu.make_async_copy(res_v, res_out, out_sem.at[0])
     res_write.start()
 
     @pl.when(owner)
@@ -271,31 +271,60 @@
             whole = whole + from_y[n]
         sums[2] = whole * (1.0 / (2 * ny))
         b_copies(lambda c: c.start(), lambda xr: sums.at[2], total, t_send, t_recv)
-        total[rows16(half), half_cols(xl)] = sums[2]
+        mine = pltpu.make_async_copy(sums.at[2], total.at[rows16(half), half_cols(xl)], out_sem.at[1])
+        mine.start()
+        mine.wait()
 
     b_wait(total, t_send, t_recv)
-    update = invert(total[...])
-    for c in range(chunks):
+    a_copies(lambda c: c.wait_send())
+
+    @pl.when(owner)
+    def _():
+        y_copies(lambda c: c.wait_send())
+        b_copies(lambda c: c.wait_send(), lambda xr: sums.at[xr], band, b_send, b_recv)
+        b_copies(lambda c: c.wait_send(), lambda xr: sums.at[2], total, t_send, t_recv)
+
+    res_write.wait()
+
+
+def finish(
+    cols,
+    total_in, res_in, outer_in, mom_in, coli_in, rowi_in,
+    outer_out, mom_out, res_out,
+    total, outer_v, mom_v, coli, rowi, load_sem, out_sem,
+):
+    d = lax.rem(lax.axis_index("fsdp"), RING)
+    two = lax.div(3 * d, 8) != lax.div(3 * d + 2, 8)
+    writes = [
+        pltpu.make_async_copy(src, dst, out_sem.at[n])
+        for n, (src, dst) in enumerate([(res_in, res_out.at[0]), (mom_v, mom_out), (outer_v, outer_out)])
+    ]
+    loads = [
+        pltpu.make_async_copy(src, dst, load_sem.at[n])
+        for n, (src, dst) in enumerate(
+            [(total_in, total), (rowi_in.at[d], rowi), (coli_in, coli), (mom_in, mom_v), (outer_in, outer_v)]
+        )
+    ]
+    for c in loads:
+        c.start()
+    writes[0].start()
+    loads[0].wait()
+
+    @pl.when(jnp.logical_not(two))
+    def _():
+        total[BAND:] = jnp.zeros((BAND, cols * BAND // GROUP), jnp.float32)
+
+    for c in loads[1:]:
+        c.wait()
+    update = invert(total[...], rowi[...], coli[...])
+    for c in range(cols // 512):
         at_c = slice(512 * c, 512 * (c + 1))
         u = update[ROWS_DEV * c : ROWS_DEV * (c + 1)]
         m = KEEP * mom_v[:, at_c] + u
         mom_v[:, at_c] = m
         outer_v[:, at_c] = outer_v[:, at_c] - OUTER_RATE * (u + KEEP * m)
-    writes = [
-        pltpu.make_async_copy(mom_v, mom_out, out_sem.at[1]),
-        pltpu.make_async_copy(outer_v, outer_out, out_sem.at[2]),
-    ]
-    for c in writes:
+    for c in writes[1:]:
         c.start()
-    a_copies(lambda c: c.wait_send())
-
-    @pl.when(owner)
-    def _():
-        y_copies(lambda c: c.wait_send())
-        b_copies(lambda c: c.wait_send(), lambda xr: sums.at[xr], band, b_send, b_recv)
-        b_copies(lambda c: c.wait_send(), lambda xr: sums.at[2], total, t_send, t_recv)
-
-    res_write.wait()
     for c in writes:
         c.wait()
 
@@ -309,42 +338,56 @@
         hc = cols * BAND // GROUP // 2
         f32, bf16 = jnp.float32, jnp.bfloat16
         dma = pltpu.SemaphoreType.DMA
+        any_space = pl.BlockSpec(memory_space=pl.ANY)
+        in_hbm = lambda a: pltpu.with_memory_space_constraint(a, pltpu.HBM)
+        colf, coli, rowf, rowi = (jnp.asarray(a) for a in (col_fwd, col_inv, row_fwd, row_inv))
+        total, res_next = pl.pallas_call(
+            functools.partial(kernel, ny, cols),
+            name="exchange",
+            out_shape=[pltpu.VMEM((2 * BAND, 2 * hc), f32), pltpu.VMEM((rows, cols), f32)],
+            in_specs=[any_space] * 7,
+            out_specs=[any_space] * 2,
+            scratch_shapes=[
+                pltpu.VMEM((rows, cols), bf16),
+                pltpu.VMEM((rows, cols), f32),
+                pltpu.VMEM((rows, cols), f32),
+                pltpu.VMEM(col_fwd.shape, bf16),
+                pltpu.VMEM(col_inv.shape, bf16),
+                pltpu.VMEM(row_fwd.shape[1:], bf16),
+                pltpu.VMEM(row_inv.shape[1:], bf16),
+                pltpu.VMEM((2 * BAND, 2 * hc), f32),
+                pltpu.VMEM((8, 16, hc), f32),
+                pltpu.VMEM((3, 16, hc), f32),
+                pltpu.VMEM((ny, 16, hc), f32),
+                pltpu.VMEM((2 * BAND, 2 * hc), f32),
+                dma((7,)), dma((2,)),
+                dma((8,)), dma((8,)), dma((ny,)), dma((ny,)), dma((8,)), dma((8,)), dma((8,)), dma((8,)),
+            ],
+            compiler_params=pltpu.CompilerParams(
+                collective_id=0, has_side_effects=True, vmem_limit_bytes=24 * 1024 * 1024
+            ),
+        )(*map(in_hbm, (inner, outer, residual, colf, coli, rowf, rowi)))
         return tuple(
             pl.pallas_call(
-                functools.partial(kernel, ny, cols),
-                name="outer_step",
+                functools.partial(finish, cols),
+                name="finish",
                 out_shape=[
                     jax.ShapeDtypeStruct((rows, cols), f32),
                     jax.ShapeDtypeStruct((rows, cols), f32),
                     jax.ShapeDtypeStruct((1, rows, cols), f32),
                 ],
-                in_specs=[pl.BlockSpec(memory_space=pltpu.HBM)] * 8,
-                out_specs=[pl.BlockSpec(memory_space=pl.ANY)] * 3,
+                in_specs=[any_space] * 6,
+                out_specs=[any_space] * 3,
                 scratch_shapes=[
-                    pltpu.VMEM((rows, cols), bf16),
+                    pltpu.VMEM((2 * BAND, 2 * hc), f32),
                     pltpu.VMEM((rows, cols), f32),
                     pltpu.VMEM((rows, cols), f32),
-                    pltpu.VMEM((rows, cols), f32),
-                    pltpu.VMEM(col_fwd.shape, bf16),
                     pltpu.VMEM(col_inv.shape, bf16),
-                    pltpu.VMEM(row_fwd.shape[1:], bf16),
                     pltpu.VMEM(row_inv.shape[1:], bf16),
-                    pltpu.VMEM((2 * BAND, 2 * hc), f32),
-                    pltpu.VMEM((8, 16, hc), f32),
-                    pltpu.VMEM((3, 16, hc), f32),
-                    pltpu.VMEM((ny, 16, hc), f32),
-                    pltpu.VMEM((2 * BAND, 2 * hc), f32),
-                    pltpu.VMEM((2 * BAND, 2 * hc), f32),
-                    dma((8,)), dma((3,)),
-                    dma((8,)), dma((8,)), dma((ny,)), dma((ny,)), dma((8,)), dma((8,)), dma((8,)), dma((8,)),
+                    dma((5,)), dma((3,)),
                 ],
-                compiler_params=pltpu.CompilerParams(
-                    collective_id=0, has_side_effects=True, vmem_limit_bytes=40 * 1024 * 1024
-                ),
-            )(
-                inner, outer, momentum, residual,
-                jnp.asarray(col_fwd), jnp.asarray(col_inv), jnp.asarray(row_fwd), jnp.asarray(row_inv),
-            )
+                compiler_params=pltpu.CompilerParams(vmem_limit_bytes=24 * 1024 * 1024),
+            )(total, res_next, outer, momentum, coli, rowi)
         )
 
     return jax.shard_map(

time: 37.4 us -> 28.4 us (0.76)
  local copies, waits for them, and re-layouts: 10.4 us -> 0.02 us
  Pallas kernels: 25.9 us -> 27.5 us
    unnamed x19 -> x8, local copies, waits for them, and re-layouts: 10.4 us -> 0.02 us
    pallas_call x1 -> x2, Pallas kernels: 25.9 us -> 27.5 us  [the longest x1 25.2 us: per_device(): pl.pallas_call(functools.partial(kernel, ny, cols), name='exchange', out_...]
where the time goes in v2:
time: 28.4 us; the launch traced here: 28.2 us
  Pallas kernels  27.5 us (97%)
  between operations  0.7 us (2%)
    pallas_call x1, Pallas kernels, per_device(): pl.pallas_call(functools.partial(kernel, ny, cols), name='exchange', out_...  25.2 us
    pallas_call x1, Pallas kernels, per_device(): pl.pallas_call(functools.partial(finish, cols), name='finish', out_shape=...  2.28 us

profile of v2, /device:TPU:1, one launch (start us, length us, event | category | flops | bytes accessed | tf_op | source)
XLA Modules:
  0.0 28.2 jit_solution(17331087833790239447)
XLA Ops:
  0.6 0.0 copy-start.1
  0.6 0.0 copy-start.2
  0.7 0.0 copy-start
  0.7 0.0 copy-start.3
  0.7 25.2 %exchange.1 = (f32[64,768]{1,0:T(8,128)S(1)}, f32[48,3072]{1,0:T(8,128)S(1)}) custom-call(bf16[1,48,3072]{2,1,0:T(8,128)(2,1)} %inner_in.1, f32[48,3072]{1,0:T(8,128)} %outer_in.3, f32[1,48,3072]{2,1,0:T(8,128)} %res_in.1, bf16[512,256]{1,0:T(8,128)(2,1)} %constant.8.clone.colf_in, bf16[384,512]{1,0:T(8,128)(2,1)} %constant.9.clone.coli_in, ...), custom_call_target="tpu_custom_call" | custom-call | tf_op jit(solution)/shard_map/exchange/pallas_call | solution.py:344
  25.9 0.0 copy-done.1
  25.9 0.0 copy-done.2
  25.9 0.0 copy-done
  26.0 0.0 copy-done.3
  26.0 2.3 %finish.1 = (f32[48,3072]{1,0:T(8,128)}, f32[48,3072]{1,0:T(8,128)}, f32[1,48,3072]{2,1,0:T(8,128)}) custom-call(f32[64,768]{1,0:T(8,128)S(1)} %get-tuple-element.5.total_in, f32[48,3072]{1,0:T(8,128)S(1)} %get-tuple-element.6.res_in, f32[48,3072]{1,0:T(8,128)S(1)} %copy-done, f32[48,3072]{1,0:T(8,128)S(1)} %copy-done.3, bf16[384,512]{1,0:T(8,128)(2,1)S(1)} %copy-done.1, ...), custom_call_target="tpu_custom_call" | custom-call | tf_op jit(solution)/shard_map/finish/pallas_call | solution.py:371
Async XLA Ops:
  0.6 25.3 %copy-start.1 = (bf16[384,512]{1,0:T(8,128)(2,1)S(1)}, bf16[384,512]{1,0:T(8,128)(2,1)}, u32[]{:S(2)}) copy-start(bf16[384,512]{1,0:T(8,128)(2,1)} %constant.9.clone.coli_in) | copy-start | bytes 1179652
  0.6 25.3 %copy-start.2 = (bf16[8,48,192]{2,1,0:T(8,128)(2,1)S(1)}, bf16[8,48,192]{2,1,0:T(8,128)(2,1)}, u32[]{:S(2)}) copy-start(bf16[8,48,192]{2,1,0:T(8,128)(2,1)} %constant.11.clone.rowi_in) | copy-start | bytes 442372
  0.7 25.3 %copy-start = (f32[48,3072]{1,0:T(8,128)S(1)}, f32[48,3072]{1,0:T(8,128)}, u32[]{:S(2)}) copy-start(f32[48,3072]{1,0:T(8,128)} %outer_in.3) | copy-start | bytes 1769476
  0.7 25.3 %copy-start.3 = (f32[48,3072]{1,0:T(8,128)S(1)}, f32[48,3072]{1,0:T(8,128)}, u32[]{:S(2)}) copy-start(f32[48,3072]{1,0:T(8,128)} %mom_in.1) | copy-start | bytes 1769476

commit v3 on v2

v3 whole, which is shorter than its diff:
```python
import functools

import jax
import jax.numpy as jnp
import ml_dtypes
import numpy as np
from jax import lax
from jax.experimental import pallas as pl
from jax.experimental.pallas import tpu as pltpu
from jax.sharding import PartitionSpec as P

GROUP = 128
BAND = 32
ROWS_DEV = 48
RING = 8
OUTER_RATE = 0.7
KEEP = 0.9
MESH = pl.DeviceIdType.MESH
BF16 = ml_dtypes.bfloat16


def split_np(a):
    hi = a.astype(np.float32).astype(BF16)
    lo = (a - hi.astype(np.float64)).astype(np.float32).astype(BF16)
    return hi, lo


def cosine_low():
    freq = np.arange(BAND, dtype=np.float64)[:, None]
    place = np.arange(GROUP, dtype=np.float64)[None, :]
    table = np.cos(np.pi * (2.0 * place + 1.0) * freq / (2.0 * GROUP))
    scale = np.where(freq == 0, np.sqrt(1.0 / GROUP), np.sqrt(2.0 / GROUP))
    return table * scale


def tables():
    low = cosine_low()
    diag = np.zeros((4 * GROUP, 4 * BAND))
    for q in range(4):
        diag[q * GROUP : (q + 1) * GROUP, q * BAND : (q + 1) * BAND] = low.T
    hi, lo = split_np(diag)
    col_fwd = np.concatenate([hi, lo], axis=1)
    hi, lo = split_np(diag.T)
    col_inv = np.concatenate([hi, hi, lo], axis=0)
    row_fwd = np.zeros((RING, 2 * BAND, 3 * ROWS_DEV), BF16)
    row_inv = np.zeros((RING, ROWS_DEV, 3 * 2 * BAND), BF16)
    for d in range(RING):
        rows = d * ROWS_DEV + np.arange(ROWS_DEV)
        first, last = rows[0] // GROUP, rows[-1] // GROUP
        part = np.zeros((2 * BAND, ROWS_DEV))
        for slot, b in enumerate((first, last)):
            if slot == 1 and first == last:
                continue
            inside = rows // GROUP == b
            part[slot * BAND : (slot + 1) * BAND, inside] = low[:, rows[inside] % GROUP]
        hi, lo = split_np(part)
        row_fwd[d] = np.concatenate([hi, hi, lo], axis=1)
        hi, lo = split_np(part.T)
        row_inv[d] = np.concatenate([hi, hi, lo], axis=1)
    return col_fwd, col_inv, row_fwd, row_inv


def split(a):
    hi = a.astype(jnp.bfloat16)
    lo = (a - hi.astype(jnp.float32)).astype(jnp.bfloat16)
    return hi, lo


def dot(a, b):
    return jnp.dot(a, b, preferred_element_type=jnp.float32)


def invert(coef, rowi, coli):
    hi, lo = split(coef)
    wide = dot(rowi, jnp.concatenate([hi, lo, hi], axis=0))
    tall = jnp.concatenate([wide[:, 128 * c : 128 * (c + 1)] for c in range(wide.shape[1] // 128)], axis=0)
    hi, lo = split(tall)
    return dot(jnp.concatenate([hi, lo, hi], axis=1), coli)


def kernel(
    ny, cols,
    inner_in, outer_in, mom_in, res_in, colf_in, coli_in, rowf_in, rowi_in,
    total, res, outer, mom, coli, rowi,
    inner, colf, rowf, part, from_a, sums, from_y, band,
    load_sem, own_sem, up_sem, ring_sem,
    a_send, a_recv, y_send, y_recv, b_send, b_recv, t_send, t_recv,
):
    hc = cols * BAND // GROUP // 2
    wide = cols // 2
    i, f = lax.axis_index("island"), lax.axis_index("fsdp")
    y, xl = lax.div(i, 2), lax.rem(i, 2)
    d = lax.rem(f, RING)
    base = f - d
    lo_b, hi_b = lax.div(3 * d, 8), lax.div(3 * d + 2, 8)
    first = lambda b: lax.div(8 * b, 3)
    last = lambda b: lax.div(8 * b + 7, 3)
    own_b, half = lax.div(d, 3), lax.rem(d, 3)
    owner = half != 2
    two = lo_b != hi_b
    prim = jnp.where(d == RING - 3, 1, 0)
    prim_b = jnp.where(prim == 1, hi_b, lo_b)

    def at(yy, xx, dd):
        return (yy * 2 + xx, base + dd)

    def signal(sem, where):
        pl.semaphore_signal(sem, 1, device_id=where, device_id_type=MESH)

    def half_of(r):
        return lax.rem(xl + 1 + r, 2)

    def wide_cols(r):
        return pl.ds(pl.multiple_of(half_of(r) * wide, 128), wide)

    loads = []

    def load(src, dst):
        loads.append(pltpu.make_async_copy(src, dst, load_sem.at[len(loads)]))
        loads[-1].start()

    load(inner_in.at[0, :, wide_cols(0)], inner.at[0])
    load(res_in.at[0, :, wide_cols(0)], res.at[0])
    load(outer_in.at[:, wide_cols(0)], outer.at[0])
    load(colf_in, colf)

    bar = pltpu.get_barrier_semaphore()
    x2 = 1 - xl
    for m in range(3):
        to_d = jnp.where(prim_b == 1, 3 + m, first(prim_b) + m)
        for xr in range(2):
            @pl.when(((to_d != d) | (xr == 1)) & ((prim_b != 1) | (m < 2)))
            def _():
                signal(bar, at(y, lax.rem(xl + xr, 2), to_d))

    @pl.when(two)
    def _():
        for m in range(2):
            for xr in range(2):
                signal(bar, at(y, lax.rem(xl + xr, 2), 3 + m))

    @pl.when(owner)
    def _():
        for k in (1, 2, ny - 1, ny - 2):
            signal(bar, at(lax.rem(y + k, ny), xl, d))

    load(inner_in.at[0, :, wide_cols(1)], inner.at[1])
    load(res_in.at[0, :, wide_cols(1)], res.at[1])
    load(outer_in.at[:, wide_cols(1)], outer.at[1])
    load(rowf_in.at[d], rowf)

    @pl.when(own_b != 1)
    def _():
        from_a[6:8] = jnp.zeros((2, 16, hc), jnp.float32)

    @pl.when(jnp.logical_not(two))
    def _():
        band[:, BAND:] = jnp.zeros((2, BAND, hc), jnp.float32)
        total[BAND:] = jnp.zeros((BAND, 2 * hc), jnp.float32)

    chunks = wide // 512

    def forward(r):
        acc = outer[r] - inner[r].astype(jnp.float32) + res[r]
        res[r] = acc
        hi, lo = split(jnp.concatenate([acc[:, 512 * c : 512 * (c + 1)] for c in range(chunks)], axis=0))
        prod = dot(hi, colf[...])
        tall = prod[:, :128] + prod[:, 128:] + dot(lo, colf[:, :128])
        hi, lo = split(jnp.concatenate([tall[ROWS_DEV * c : ROWS_DEV * (c + 1)] for c in range(chunks)], axis=1))
        part[r] = dot(rowf[...], jnp.concatenate([hi, lo, hi], axis=0))

    def rows16(n):
        return pl.ds(pl.multiple_of(n * 16, 16), 16)

    def half_cols(xx):
        return pl.ds(pl.multiple_of(xx * hc, 128), hc)

    def a_copies(run, r, second):
        slot = 1 - prim if second else prim
        b = 1 if second else prim_b
        for h in range(2):
            to_d = 3 * b + h

            def go():
                run(
                    pltpu.make_async_remote_copy(
                        part.at[r, rows16(slot * 2 + h)],
                        from_a.at[(d - first(b)) * 2 + xl],
                        a_send.at[second * 4 + h * 2 + r],
                        a_recv.at[(d - first(b)) * 2 + xl],
                        device_id=at(y, half_of(r), to_d),
                        device_id_type=MESH,
                    )
                )

            if second or r == 0:
                go()
            else:
                pl.when(to_d != d)(go)

    for c in loads[:4]:
        c.wait()
    loads[7].wait()
    forward(0)
    pl.semaphore_wait(bar, jnp.where(two, 5, jnp.where(own_b == 1, 11, 9)))

    a_copies(lambda c: c.start(), 0, False)

    @pl.when((d == 3) | (d == 4))
    def _():
        signal(up_sem, at(y, xl, jnp.where(d == 3, 2, 5)))

    @pl.when(owner)
    def _():
        for k in (2, ny - 2):
            signal(ring_sem, at(lax.rem(y + k, ny), xl, d))

    for c in loads[4:7]:
        c.wait()
    forward(1)
    a_copies(lambda c: c.start(), 1, False)

    @pl.when(two)
    def _():
        pl.semaphore_wait(up_sem, 1)
        a_copies(lambda c: c.start(), 0, True)
        a_copies(lambda c: c.start(), 1, True)

    load(coli_in, coli)
    load(rowi_in.at[d], rowi)
    load(mom_in, mom)

    me_a = (d - first(own_b)) * 2 + xl

    def dummy(ref, send, recv):
        return pltpu.make_async_remote_copy(ref, ref, send, recv, device_id=at(y, x2, d), device_id_type=MESH)

    def y_copies(run):
        for k in (4, 3, 5, 2, 6, 1, 7):
            run(
                pltpu.make_async_remote_copy(
                    from_y.at[y], from_y.at[y], y_send.at[k], y_recv.at[y],
                    device_id=at(lax.rem(y + k, ny), xl, d), device_id_type=MESH,
                )
            )

    def b_copies(run, src, dst, send, recv):
        for m in range(4):
            to_d = first(own_b) + m
            slot = own_b - lax.div(3 * to_d, 8)
            for xr in range(2):
                @pl.when((to_d <= last(own_b)) & ((to_d != d) | (xr == 1)))
                def _():
                    run(
                        pltpu.make_async_remote_copy(
                            src(xr),
                            dst(slot * 2 + half, xr),
                            send.at[m * 2 + xr],
                            recv.at[slot * 4 + half * 2 + 1 - xr],
                            device_id=at(y, lax.rem(xl + xr, 2), to_d),
                            device_id_type=MESH,
                        )
                    )

    def b_wait(send, recv):
        for slot in range(2):
            for h in range(2):
                for r in range(2):
                    n = slot * 4 + h * 2 + r

                    @pl.when(two if slot == 1 else ((3 * lo_b + h != d) | (r == 0)))
                    def _():
                        dummy(sums.at[0], send.at[n], recv.at[n]).wait_recv()

    band_at = lambda n, xr: band.at[1 - xr, rows16(n)]
    total_at = lambda n, xr: total.at[rows16(n), half_cols(xl)]

    @pl.when(owner)
    def _():
        from_a[me_a] = part[1, rows16(half)]
        for n in range(8):
            @pl.when((n != me_a) & (first(own_b) + n // 2 <= last(own_b)))
            def _():
                dummy(from_a.at[n], a_send.at[n], a_recv.at[n]).wait_recv()

        def add(x):
            return (from_a[x] + from_a[2 + x]) + (from_a[4 + x] + from_a[6 + x])

        mine, other = add(xl), add(1 - xl)
        sums[0] = mine
        sums[1] = other
        from_y[y] = mine + other
        pl.semaphore_wait(ring_sem, 2)
        y_copies(lambda c: c.start())
        b_copies(lambda c: c.start(), lambda xr: sums.at[xr], band_at, b_send, b_recv)
        band[1, rows16(half)] = mine

    for c in loads[8:]:
        c.wait()

    b_wait(b_send, b_recv)
    sent = invert(jnp.concatenate([band[0], band[1]], axis=1), rowi[...], coli[...])
    for c in range(2 * chunks):
        r, at_c = c // chunks, slice(512 * (c % chunks), 512 * (c % chunks + 1))
        res[r, :, at_c] = res[r, :, at_c] - sent[ROWS_DEV * c : ROWS_DEV * (c + 1)]

    @pl.when(owner)
    def _():
        for k in range(1, ny):
            n = lax.rem(y + k, ny)
            dummy(from_y.at[n], y_send.at[k], y_recv.at[n]).wait_recv()
        whole = from_y[0]
        for n in range(1, ny):
            whole = whole + from_y[n]
        sums[2] = whole * (1.0 / (2 * ny))
        b_copies(lambda c: c.start(), lambda xr: sums.at[2], total_at, t_send, t_recv)
        total[rows16(half), half_cols(xl)] = sums[2]

    for r in range(2):
        a_copies(lambda c: c.wait_send(), r, False)

    @pl.when(two)
    def _():
        for r in range(2):
            a_copies(lambda c: c.wait_send(), r, True)

    @pl.when(owner)
    def _():
        y_copies(lambda c: c.wait_send())
        b_copies(lambda c: c.wait_send(), lambda xr: sums.at[xr], band_at, b_send, b_recv)

    b_wait(t_send, t_recv)

    @pl.when(owner)
    def _():
        b_copies(lambda c: c.wait_send(), lambda xr: sums.at[2], total_at, t_send, t_recv)


def finish(
    cols,
    total, res, outer, mom, coli, rowi,
    outer_out, mom_out, res_out,
    outer_v, mom_v, out_sem,
):
    xl = lax.rem(lax.axis_index("island"), 2)
    wide = cols // 2
    writes = []

    def write(src, dst):
        writes.append(pltpu.make_async_copy(src, dst, out_sem.at[len(writes)]))
        writes[-1].start()

    def columns(r, n, width):
        return pl.ds(pl.multiple_of(lax.rem(xl + 1 + r, 2) * wide + n, 128), width)

    for r in range(2):
        write(res.at[r], res_out.at[0, :, columns(r, 0, wide)])
    hi, lo = split(total[...])
    half = dot(rowi[...], jnp.concatenate([hi, lo, hi], axis=0))
    step = 1024
    for c in range(cols // step):
        at_c = slice(step * c, step * (c + 1))
        tall = jnp.concatenate([half[:, 128 * q : 128 * (q + 1)] for q in range(c * step // 512, (c + 1) * step // 512)], axis=0)
        hi, lo = split(tall)
        update = dot(jnp.concatenate([hi, lo, hi], axis=1), coli[...])
        for q in range(step // 512):
            n = (c * step + 512 * q) % wide
            r = (c * step + 512 * q) // wide
            at_q = slice(step * c + 512 * q, step * c + 512 * (q + 1))
            u = update[ROWS_DEV * q : ROWS_DEV * (q + 1)]
            rel = jnp.where(r == xl, 1, 0)
            m = KEEP * mom[:, at_q] + u
            mom_v[:, at_q] = m
            outer_v[:, at_q] = outer[rel, :, n : n + 512] - OUTER_RATE * (u + KEEP * m)
        write(mom_v.at[:, at_c], mom_out.at[:, at_c])
        write(outer_v.at[:, at_c], outer_out.at[:, at_c])
    for c in writes:
        c.wait()


def solution(mesh):
    ny = mesh.shape["island"] // 2
    col_fwd, col_inv, row_fwd, row_inv = tables()

    def per_device(inner, outer, momentum, residual):
        rows, cols = outer.shape
        hc = cols * BAND // GROUP // 2
        f32, bf16 = jnp.float32, jnp.bfloat16
        dma, regular = pltpu.SemaphoreType.DMA, pltpu.SemaphoreType.REGULAR
        any_space = pl.BlockSpec(memory_space=pl.ANY)
        vmem = pl.BlockSpec(memory_space=pltpu.VMEM)
        in_hbm = lambda a: pltpu.with_memory_space_constraint(a, pltpu.HBM)
        tables_hbm = [jnp.asarray(a) for a in (col_fwd, col_inv, row_fwd, row_inv)]
        passed = pl.pallas_call(
            functools.partial(kernel, ny, cols),
            name="exchange",
            out_shape=[
                pltpu.VMEM((2 * BAND, 2 * hc), f32),
                pltpu.VMEM((2, rows, cols // 2), f32),
                pltpu.VMEM((2, rows, cols // 2), f32),
                pltpu.VMEM((rows, cols), f32),
                pltpu.VMEM(col_inv.shape, bf16),
                pltpu.VMEM(row_inv.shape[1:], bf16),
            ],
            in_specs=[any_space] * 8,
            out_specs=[vmem] * 6,
            scratch_shapes=[
                pltpu.VMEM((2, rows, cols // 2), bf16),
                pltpu.VMEM(col_fwd.shape, bf16),
                pltpu.VMEM(row_fwd.shape[1:], bf16),
                pltpu.VMEM((2, 2 * BAND, hc), f32),
                pltpu.VMEM((8, 16, hc), f32),
                pltpu.VMEM((3, 16, hc), f32),
                pltpu.VMEM((ny, 16, hc), f32),
                pltpu.VMEM((2, 2 * BAND, hc), f32),
                dma((11,)), dma((1,)), regular, regular,
                dma((8,)), dma((8,)), dma((ny,)), dma((ny,)), dma((8,)), dma((8,)), dma((8,)), dma((8,)),
            ],
            compiler_params=pltpu.CompilerParams(
                collective_id=0, has_side_effects=True, vmem_limit_bytes=24 * 1024 * 1024
            ),
        )(*map(in_hbm, (inner, outer, momentum, residual, *tables_hbm)))
        return tuple(
            pl.pallas_call(
                functools.partial(finish, cols),
                name="finish",
                out_shape=[
                    jax.ShapeDtypeStruct((rows, cols), f32),
                    jax.ShapeDtypeStruct((rows, cols), f32),
                    jax.ShapeDtypeStruct((1, rows, cols), f32),
                ],
                in_specs=[vmem] * 6,
                out_specs=[any_space] * 3,
                scratch_shapes=[pltpu.VMEM((rows, cols), f32), pltpu.VMEM((rows, cols), f32), dma((8,))],
                compiler_params=pltpu.CompilerParams(vmem_limit_bytes=24 * 1024 * 1024),
            )(*passed)
        )

    return jax.shard_map(
        per_device,
        mesh=mesh,
        in_specs=(P("island", "fsdp", None), P("fsdp", None), P("fsdp", None), P("island", "fsdp", None)),
        out_specs=(P("fsdp", None), P("fsdp", None), P("island", "fsdp", None)),
        check_vma=False,
    )
```

time: 28.4 us -> 24.5 us (0.86)
  Pallas kernels: 27.5 us -> 23.7 us
    pallas_call x1, Pallas kernels: 25.2 us -> 22.2 us  [per_device(): pl.pallas_call(functools.partial(kernel, ny, cols), name='exchange', out_...]
    pallas_call x1, Pallas kernels: 2.28 us -> 1.43 us  [per_device(): pl.pallas_call(functools.partial(finish, cols), name='finish', out_shape=...]
where the time goes in v3:
time: 24.5 us; the launch traced here: 24.3 us
  Pallas kernels  23.7 us (97%)
  between operations  0.64 us (3%)
    pallas_call x1, Pallas kernels, per_device(): pl.pallas_call(functools.partial(kernel, ny, cols), name='exchange', out_...  22.2 us
    pallas_call x1, Pallas kernels, per_device(): pl.pallas_call(functools.partial(finish, cols), name='finish', out_shape=...  1.43 us

profile of v3, /device:TPU:1, one launch (start us, length us, event | category | flops | bytes accessed | tf_op | source)
XLA Modules:
  0.0 24.3 jit_solution(5948203002243170381)
XLA Ops:
  0.6 22.2 %exchange.1 = (f32[64,768]{1,0:T(8,128)S(1)}, f32[2,48,1536]{2,1,0:T(8,128)S(1)}, f32[2,48,1536]{2,1,0:T(8,128)S(1)}, f32[48,3072]{1,0:T(8,128)S(1)}, bf16[384,5...) custom-call(bf16[1,48,3072]{2,1,0:T(8,128)(2,1)} %inner_in.1, f32[48,3072]{1,0:T(8,128)} %outer_in.1, f32[48,3072]{1,0:T(8,128)} %mom_in.1, ...), custom_call_target="tpu_custom_call" | custom-call | tf_op jit(solution)/shard_map/exchange/pallas_call | solution.py:394
  22.9 1.4 %finish.1 = (f32[48,3072]{1,0:T(8,128)}, f32[48,3072]{1,0:T(8,128)}, f32[1,48,3072]{2,1,0:T(8,128)}) custom-call(f32[64,768]{1,0:T(8,128)S(1)} %get-tuple-element.9.total, f32[2,48,1536]{2,1,0:T(8,128)S(1)} %get-tuple-element.10.res, f32[2,48,1536]{2,1,0:T(8,128)S(1)} %get-tuple-element.11.outer, f32[48,3072]{1,0:T(8,128)S(1)} %get-tuple-element.12.mom, ...), custom_call_target="tpu_custom_call" | custom-call | tf_op jit(solution)/shard_map/finish/pallas_call | solution.py:424

commit v4 on v3

--- a/solution.py
+++ b/solution.py
@@ -78,12 +78,25 @@
     return dot(jnp.concatenate([hi, lo, hi], axis=1), coli)
 
 
+OWNS = {1: (0, 0, 24), 2: (0, 24, 8), 3: (1, 0, 16), 4: (1, 16, 16), 5: (2, 0, 8), 6: (2, 8, 24)}
+MEMBERS = ((0, 1, 2), (2, 3, 4, 5), (5, 6, 7))
+MOST = 24
+
+
+def blocks_of(d):
+    return [b for b in range(3) if d in MEMBERS[b]]
+
+
+def owners_of(b):
+    return [d for d in OWNS if OWNS[d][0] == b]
+
+
 def kernel(
     ny, cols,
     inner_in, outer_in, mom_in, res_in, colf_in, coli_in, rowf_in, rowi_in,
     total, res, outer, mom, coli, rowi,
     inner, colf, rowf, part, from_a, sums, from_y, band,
-    load_sem, own_sem, up_sem, ring_sem,
+    load_sem, up_sem, ring_sem,
     a_send, a_recv, y_send, y_recv, b_send, b_recv, t_send, t_recv,
 ):
     hc = cols * BAND // GROUP // 2
@@ -92,26 +105,22 @@
     y, xl = lax.div(i, 2), lax.rem(i, 2)
     d = lax.rem(f, RING)
     base = f - d
-    lo_b, hi_b = lax.div(3 * d, 8), lax.div(3 * d + 2, 8)
-    first = lambda b: lax.div(8 * b, 3)
-    last = lambda b: lax.div(8 * b + 7, 3)
-    own_b, half = lax.div(d, 3), lax.rem(d, 3)
-    owner = half != 2
-    two = lo_b != hi_b
-    prim = jnp.where(d == RING - 3, 1, 0)
-    prim_b = jnp.where(prim == 1, hi_b, lo_b)
-
-    def at(yy, xx, dd):
-        return (yy * 2 + xx, base + dd)
+
+    def at(yy, xr, dd):
+        return (yy * 2 + (1 - xl if xr else xl), base + dd)
+
+    def ring(k):
+        return lax.rem(y + k, ny)
 
     def signal(sem, where):
         pl.semaphore_signal(sem, 1, device_id=where, device_id_type=MESH)
 
-    def half_of(r):
-        return lax.rem(xl + 1 + r, 2)
+    def each(devices, body):
+        for dd in devices:
+            pl.when(d == dd)(functools.partial(body, dd))
 
     def wide_cols(r):
-        return pl.ds(pl.multiple_of(half_of(r) * wide, 128), wide)
+        return pl.ds(pl.multiple_of((xl if r else 1 - xl) * wide, 128), wide)
 
     loads = []
 
@@ -125,35 +134,27 @@
     load(colf_in, colf)
 
     bar = pltpu.get_barrier_semaphore()
-    x2 = 1 - xl
-    for m in range(3):
-        to_d = jnp.where(prim_b == 1, 3 + m, first(prim_b) + m)
-        for xr in range(2):
-            @pl.when(((to_d != d) | (xr == 1)) & ((prim_b != 1) | (m < 2)))
-            def _():
-                signal(bar, at(y, lax.rem(xl + xr, 2), to_d))
-
-    @pl.when(two)
-    def _():
-        for m in range(2):
+
+    def greet(dd):
+        for m in MEMBERS[OWNS[dd][0]]:
+            if OWNS[dd][0] == 1 and m in (2, 5):
+                continue
             for xr in range(2):
-                signal(bar, at(y, lax.rem(xl + xr, 2), 3 + m))
-
-    @pl.when(owner)
-    def _():
-        for k in (1, 2, ny - 1, ny - 2):
-            signal(bar, at(lax.rem(y + k, ny), xl, d))
+                if (m, xr) != (dd, 0):
+                    signal(bar, at(y, xr, m))
+        if dd in (2, 5):
+            signal(bar, at(y, 0, 3 if dd == 2 else 4))
+        for k in (1, ny - 1, 2, ny - 2):
+            signal(bar, at(ring(k), 0, dd))
+
+    each(OWNS, greet)
 
     load(inner_in.at[0, :, wide_cols(1)], inner.at[1])
     load(res_in.at[0, :, wide_cols(1)], res.at[1])
     load(outer_in.at[:, wide_cols(1)], outer.at[1])
     load(rowf_in.at[d], rowf)
 
-    @pl.when(own_b != 1)
-    def _():
-        from_a[6:8] = jnp.zeros((2, 16, hc), jnp.float32)
-
-    @pl.when(jnp.logical_not(two))
+    @pl.when((d != 2) & (d != 5))
     def _():
         band[:, BAND:] = jnp.zeros((2, BAND, hc), jnp.float32)
         total[BAND:] = jnp.zeros((BAND, 2 * hc), jnp.float32)
@@ -169,171 +170,156 @@
         hi, lo = split(jnp.concatenate([tall[ROWS_DEV * c : ROWS_DEV * (c + 1)] for c in range(chunks)], axis=1))
         part[r] = dot(rowf[...], jnp.concatenate([hi, lo, hi], axis=0))
 
-    def rows16(n):
-        return pl.ds(pl.multiple_of(n * 16, 16), 16)
-
-    def half_cols(xx):
-        return pl.ds(pl.multiple_of(xx * hc, 128), hc)
-
-    def a_copies(run, r, second):
-        slot = 1 - prim if second else prim
-        b = 1 if second else prim_b
-        for h in range(2):
-            to_d = 3 * b + h
-
-            def go():
-                run(
-                    pltpu.make_async_remote_copy(
-                        part.at[r, rows16(slot * 2 + h)],
-                        from_a.at[(d - first(b)) * 2 + xl],
-                        a_send.at[second * 4 + h * 2 + r],
-                        a_recv.at[(d - first(b)) * 2 + xl],
-                        device_id=at(y, half_of(r), to_d),
-                        device_id_type=MESH,
-                    )
-                )
-
-            if second or r == 0:
-                go()
-            else:
-                pl.when(to_d != d)(go)
+    def half_cols():
+        return pl.ds(pl.multiple_of(xl * hc, 128), hc)
+
+    def wait_rows(send, recv, rows, count=1):
+        ref = part.at[0, :rows] if count == 1 else from_a.at[:count, :rows]
+        sems = (send, send) if recv is None else (recv, recv)
+        copy = pltpu.make_async_remote_copy(ref, ref, *sems, device_id=at(y, 1, d), device_id_type=MESH)
+        copy.wait_recv() if recv is not None else copy.wait_send()
+
+    def a_send_half(dd, r, b):
+        slot = blocks_of(dd).index(b)
+        for to in owners_of(b):
+            if (to, r) == (dd, 1):
+                continue
+            row, rows = OWNS[to][1:]
+            pltpu.make_async_remote_copy(
+                part.at[r, slot * BAND + row : slot * BAND + row + rows],
+                from_a.at[MEMBERS[b].index(dd) * 2 + 1 - r, :rows],
+                a_send,
+                a_recv,
+                device_id=at(y, 1 - r, to),
+                device_id_type=MESH,
+            ).start()
+
+    def first_block(dd):
+        return 2 if dd == 5 else blocks_of(dd)[0]
 
     for c in loads[:4]:
         c.wait()
     loads[7].wait()
     forward(0)
-    pl.semaphore_wait(bar, jnp.where(two, 5, jnp.where(own_b == 1, 11, 9)))
-
-    a_copies(lambda c: c.start(), 0, False)
+    pl.semaphore_wait(bar, jnp.where((d == 0) | (d == 7), 4, jnp.where((d == 3) | (d == 4), 8, 7)))
+    each(range(RING), lambda dd: a_send_half(dd, 0, first_block(dd)))
 
     @pl.when((d == 3) | (d == 4))
     def _():
-        signal(up_sem, at(y, xl, jnp.where(d == 3, 2, 5)))
-
-    @pl.when(owner)
+        signal(up_sem, at(y, 0, jnp.where(d == 3, 2, 5)))
+
+    @pl.when((d != 0) & (d != 7))
     def _():
         for k in (2, ny - 2):
-            signal(ring_sem, at(lax.rem(y + k, ny), xl, d))
+            signal(ring_sem, at(ring(k), 0, d))
 
     for c in loads[4:7]:
         c.wait()
     forward(1)
-    a_copies(lambda c: c.start(), 1, False)
-
-    @pl.when(two)
-    def _():
-        pl.semaphore_wait(up_sem, 1)
-        a_copies(lambda c: c.start(), 0, True)
-        a_copies(lambda c: c.start(), 1, True)
+
+    def a_rest(dd):
+        a_send_half(dd, 1, first_block(dd))
+        if dd in (2, 5):
+            pl.semaphore_wait(up_sem, 1)
+            for r in range(2):
+                a_send_half(dd, r, 1)
+
+    each(range(RING), a_rest)
 
     load(coli_in, coli)
     load(rowi_in.at[d], rowi)
     load(mom_in, mom)
 
-    me_a = (d - first(own_b)) * 2 + xl
-
-    def dummy(ref, send, recv):
-        return pltpu.make_async_remote_copy(ref, ref, send, recv, device_id=at(y, x2, d), device_id_type=MESH)
-
-    def y_copies(run):
+    def b_copies(dd, src, dst, send, recv):
+        b, row, rows = OWNS[dd]
+        count = 0
+        for m in MEMBERS[b]:
+            slot = blocks_of(m).index(b)
+            for xr in (1, 0):
+                if (m, xr) != (dd, 0):
+                    count += 1
+                    pltpu.make_async_remote_copy(
+                        src(xr),
+                        dst(xr, slice(slot * BAND + row, slot * BAND + row + rows)),
+                        send,
+                        recv.at[slot],
+                        device_id=at(y, xr, m),
+                        device_id_type=MESH,
+                    ).start()
+        return count
+
+    def own_rows(dd):
+        b, row, rows = OWNS[dd]
+        start = blocks_of(dd).index(b) * BAND + row
+        return slice(start, start + rows)
+
+    def band_part(xr, at_rows):
+        return band.at[1 - xr, at_rows]
+
+    def total_part(xr, at_rows):
+        return total.at[at_rows, half_cols()]
+
+    def gather_a(dd):
+        b, row, rows = OWNS[dd]
+        wait_rows(None, a_recv, rows, 2 * len(MEMBERS[b]) - 1)
+        mine, other = part[1, own_rows(dd)], None
+        for n, m in enumerate(MEMBERS[b]):
+            if m != dd:
+                mine = mine + from_a[2 * n, :rows]
+            got = from_a[2 * n + 1, :rows]
+            other = got if other is None else other + got
+        from_y[y, :rows] = mine + other
+        sums[0, :rows] = mine
+        sums[1, :rows] = other
+        pl.semaphore_wait(ring_sem, 2)
         for k in (4, 3, 5, 2, 6, 1, 7):
-            run(
-                pltpu.make_async_remote_copy(
-                    from_y.at[y], from_y.at[y], y_send.at[k], y_recv.at[y],
-                    device_id=at(lax.rem(y + k, ny), xl, d), device_id_type=MESH,
-                )
-            )
-
-    def b_copies(run, src, dst, send, recv):
-        for m in range(4):
-            to_d = first(own_b) + m
-            slot = own_b - lax.div(3 * to_d, 8)
-            for xr in range(2):
-                @pl.when((to_d <= last(own_b)) & ((to_d != d) | (xr == 1)))
-                def _():
-                    run(
-                        pltpu.make_async_remote_copy(
-                            src(xr),
-                            dst(slot * 2 + half, xr),
-                            send.at[m * 2 + xr],
-                            recv.at[slot * 4 + half * 2 + 1 - xr],
-                            device_id=at(y, lax.rem(xl + xr, 2), to_d),
-                            device_id_type=MESH,
-                        )
-                    )
-
-    def b_wait(send, recv):
-        for slot in range(2):
-            for h in range(2):
-                for r in range(2):
-                    n = slot * 4 + h * 2 + r
-
-                    @pl.when(two if slot == 1 else ((3 * lo_b + h != d) | (r == 0)))
-                    def _():
-                        dummy(sums.at[0], send.at[n], recv.at[n]).wait_recv()
-
-    band_at = lambda n, xr: band.at[1 - xr, rows16(n)]
-    total_at = lambda n, xr: total.at[rows16(n), half_cols(xl)]
-
-    @pl.when(owner)
-    def _():
-        from_a[me_a] = part[1, rows16(half)]
-        for n in range(8):
-            @pl.when((n != me_a) & (first(own_b) + n // 2 <= last(own_b)))
-            def _():
-                dummy(from_a.at[n], a_send.at[n], a_recv.at[n]).wait_recv()
-
-        def add(x):
-            return (from_a[x] + from_a[2 + x]) + (from_a[4 + x] + from_a[6 + x])
-
-        mine, other = add(xl), add(1 - xl)
-        sums[0] = mine
-        sums[1] = other
-        from_y[y] = mine + other
-        pl.semaphore_wait(ring_sem, 2)
-        y_copies(lambda c: c.start())
-        b_copies(lambda c: c.start(), lambda xr: sums.at[xr], band_at, b_send, b_recv)
-        band[1, rows16(half)] = mine
+            pltpu.make_async_remote_copy(
+                from_y.at[y, :rows], from_y.at[y, :rows], y_send, y_recv, device_id=at(ring(k), 0, dd), device_id_type=MESH
+            ).start()
+        b_copies(dd, lambda xr: sums.at[xr, :rows], band_part, b_send, b_recv)
+        band[1, own_rows(dd)] = mine
+
+    each(OWNS, gather_a)
+
+    def b_wait(recv):
+        def go(dd):
+            for slot, b in enumerate(blocks_of(dd)):
+                wait_rows(None, recv.at[slot], 2 * BAND - (OWNS[dd][2] if dd in owners_of(b) else 0))
+
+        each(range(RING), go)
 
     for c in loads[8:]:
         c.wait()
-
-    b_wait(b_send, b_recv)
+    b_wait(b_recv)
     sent = invert(jnp.concatenate([band[0], band[1]], axis=1), rowi[...], coli[...])
     for c in range(2 * chunks):
         r, at_c = c // chunks, slice(512 * (c % chunks), 512 * (c % chunks + 1))
         res[r, :, at_c] = res[r, :, at_c] - sent[ROWS_DEV * c : ROWS_DEV * (c + 1)]
 
-    @pl.when(owner)
-    def _():
-        for k in range(1, ny):
-            n = lax.rem(y + k, ny)
-            dummy(from_y.at[n], y_send.at[k], y_recv.at[n]).wait_recv()
-        whole = from_y[0]
+    def gather_y(dd):
+        b, row, rows = OWNS[dd]
+        wait_rows(None, y_recv, rows, ny - 1)
+        whole = from_y[0, :rows]
         for n in range(1, ny):
-            whole = whole + from_y[n]
-        sums[2] = whole * (1.0 / (2 * ny))
-        b_copies(lambda c: c.start(), lambda xr: sums.at[2], total_at, t_send, t_recv)
-        total[rows16(half), half_cols(xl)] = sums[2]
-
-    for r in range(2):
-        a_copies(lambda c: c.wait_send(), r, False)
-
-    @pl.when(two)
-    def _():
-        for r in range(2):
-            a_copies(lambda c: c.wait_send(), r, True)
-
-    @pl.when(owner)
-    def _():
-        y_copies(lambda c: c.wait_send())
-        b_copies(lambda c: c.wait_send(), lambda xr: sums.at[xr], band_at, b_send, b_recv)
-
-    b_wait(t_send, t_recv)
-
-    @pl.when(owner)
-    def _():
-        b_copies(lambda c: c.wait_send(), lambda xr: sums.at[2], total_at, t_send, t_recv)
+            whole = whole + from_y[n, :rows]
+        whole = whole * (1.0 / (2 * ny))
+        sums[2, :rows] = whole
+        b_copies(dd, lambda xr: sums.at[2, :rows], total_part, t_send, t_recv)
+        total[own_rows(dd), half_cols()] = whole
+        wait_rows(y_send, None, rows, ny - 1)
+        for sem in (b_send, t_send):
+            wait_rows(sem, None, rows, 2 * len(MEMBERS[b]) - 1)
+
+    each(OWNS, gather_y)
+
+    def a_sent(dd):
+        rows = 2 * BAND - (OWNS[dd][2] if dd in OWNS else 0)
+        wait_rows(a_send, None, rows)
+        if dd in (2, 5):
+            wait_rows(a_send, None, 2 * BAND)
+
+    each(range(RING), a_sent)
+    b_wait(t_recv)
 
 
 def finish(
@@ -409,12 +395,12 @@
                 pltpu.VMEM(col_fwd.shape, bf16),
                 pltpu.VMEM(row_fwd.shape[1:], bf16),
                 pltpu.VMEM((2, 2 * BAND, hc), f32),
-                pltpu.VMEM((8, 16, hc), f32),
-                pltpu.VMEM((3, 16, hc), f32),
-                pltpu.VMEM((ny, 16, hc), f32),
+                pltpu.VMEM((8, MOST, hc), f32),
+                pltpu.VMEM((3, MOST, hc), f32),
+                pltpu.VMEM((ny, MOST, hc), f32),
                 pltpu.VMEM((2, 2 * BAND, hc), f32),
-                dma((11,)), dma((1,)), regular, regular,
-                dma((8,)), dma((8,)), dma((ny,)), dma((ny,)), dma((8,)), dma((8,)), dma((8,)), dma((8,)),
+                dma((11,)), regular, regular,
+                dma, dma, dma, dma, dma, dma((2,)), dma, dma((2,)),
             ],
             compiler_params=pltpu.CompilerParams(
                 collective_id=0, has_side_effects=True, vmem_limit_bytes=24 * 1024 * 1024

time: 24.5 us -> 22.9 us (0.935)
  the two profiles are of different devices: /device:TPU:1 before, /device:TPU:65 now
where the time goes in v4:
time: 22.9 us; the launch traced here: 22.7 us
  Pallas kernels  22 us (96%)
  between operations  0.64 us (3%)
    pallas_call x1, Pallas kernels, per_device(): pl.pallas_call(functools.partial(kernel, ny, cols), name='exchange', out_...  20.6 us
    pallas_call x1, Pallas kernels, per_device(): pl.pallas_call(functools.partial(finish, cols), name='finish', out_shape=...  1.43 us

profile of v4, /device:TPU:65, one launch (start us, length us, event | category | flops | bytes accessed | tf_op | source)
XLA Modules:
  0.0 22.7 jit_solution(13566929438908982545)
XLA Ops:
  0.6 20.6 %exchange.1 = (f32[64,768]{1,0:T(8,128)S(1)}, f32[2,48,1536]{2,1,0:T(8,128)S(1)}, f32[2,48,1536]{2,1,0:T(8,128)S(1)}, f32[48,3072]{1,0:T(8,128)S(1)}, bf16[384,5...) custom-call(bf16[1,48,3072]{2,1,0:T(8,128)(2,1)} %inner_in.1, f32[48,3072]{1,0:T(8,128)} %outer_in.1, f32[48,3072]{1,0:T(8,128)} %mom_in.1, ...), custom_call_target="tpu_custom_call" | custom-call | tf_op jit(solution)/shard_map/exchange/pallas_call | solution.py:380
  21.3 1.4 %finish.1 = (f32[48,3072]{1,0:T(8,128)}, f32[48,3072]{1,0:T(8,128)}, f32[1,48,3072]{2,1,0:T(8,128)}) custom-call(f32[64,768]{1,0:T(8,128)S(1)} %get-tuple-element.9.total, f32[2,48,1536]{2,1,0:T(8,128)S(1)} %get-tuple-element.10.res, f32[2,48,1536]{2,1,0:T(8,128)S(1)} %get-tuple-element.11.outer, f32[48,3072]{1,0:T(8,128)S(1)} %get-tuple-element.12.mom, ...), custom_call_target="tpu_custom_call" | custom-call | tf_op jit(solution)/shard_map/finish/pallas_call | solution.py:410

commit v5 on v4

--- a/solution.py
+++ b/solution.py
@@ -78,7 +78,9 @@
     return dot(jnp.concatenate([hi, lo, hi], axis=1), coli)
 
 
-OWNS = {1: (0, 0, 24), 2: (0, 24, 8), 3: (1, 0, 16), 4: (1, 16, 16), 5: (2, 0, 8), 6: (2, 8, 24)}
+OWNS = (
+    [], [(0, 0, 24)], [(0, 24, 8), (1, 0, 8)], [(1, 8, 8)], [(1, 16, 8)], [(1, 24, 8), (2, 0, 8)], [(2, 8, 24)], [],
+)
 MEMBERS = ((0, 1, 2), (2, 3, 4, 5), (5, 6, 7))
 MOST = 24
 
@@ -87,8 +89,26 @@
     return [b for b in range(3) if d in MEMBERS[b]]
 
 
-def owners_of(b):
-    return [d for d in OWNS if OWNS[d][0] == b]
+def share(d, b):
+    found = [n for n, own in enumerate(OWNS[d]) if own[0] == b]
+    return (found[0], *OWNS[d][found[0]][1:]) if found else (None, 0, 0)
+
+
+def owned(d):
+    return [own[0] for own in OWNS[d]]
+
+
+def greets(d, b, m):
+    return b in owned(d) and not (b == 1 and m in (2, 5))
+
+
+def greetings(d):
+    return sum(greets(m, b, d) for b in blocks_of(d) for m, _ in partners(d, b, (1, 0))) + (4 if OWNS[d] else 0)
+
+
+def partners(d, b, halves):
+    found = [(m, xr) for m in MEMBERS[b] for xr in halves if (m, xr) != (d, 0)]
+    return sorted(found, key=lambda p: (-abs(p[0] // 2 - d // 2) - p[1], p[0] == d, p))
 
 
 def kernel(
@@ -136,18 +156,15 @@
     bar = pltpu.get_barrier_semaphore()
 
     def greet(dd):
-        for m in MEMBERS[OWNS[dd][0]]:
-            if OWNS[dd][0] == 1 and m in (2, 5):
-                continue
-            for xr in range(2):
-                if (m, xr) != (dd, 0):
+        for b in blocks_of(dd):
+            for m, xr in partners(dd, b, (1, 0)):
+                if greets(dd, b, m):
                     signal(bar, at(y, xr, m))
-        if dd in (2, 5):
-            signal(bar, at(y, 0, 3 if dd == 2 else 4))
-        for k in (1, ny - 1, 2, ny - 2):
+
+        for k in (2, ny - 2, 1, ny - 1) if OWNS[dd] else ():
             signal(bar, at(ring(k), 0, dd))
 
-    each(OWNS, greet)
+    each(range(RING), greet)
 
     load(inner_in.at[0, :, wide_cols(1)], inner.at[1])
     load(res_in.at[0, :, wide_cols(1)], res.at[1])
@@ -174,23 +191,23 @@
         return pl.ds(pl.multiple_of(xl * hc, 128), hc)
 
     def wait_rows(send, recv, rows, count=1):
-        ref = part.at[0, :rows] if count == 1 else from_a.at[:count, :rows]
+        ref = part.at[0, :rows] if count == 1 else from_a.at[0, :count, :rows]
         sems = (send, send) if recv is None else (recv, recv)
         copy = pltpu.make_async_remote_copy(ref, ref, *sems, device_id=at(y, 1, d), device_id_type=MESH)
         copy.wait_recv() if recv is not None else copy.wait_send()
 
     def a_send_half(dd, r, b):
         slot = blocks_of(dd).index(b)
-        for to in owners_of(b):
-            if (to, r) == (dd, 1):
+        for to, xr in partners(dd, b, (1 - r,)):
+            own, row, rows = share(to, b)
+            if not rows:
                 continue
-            row, rows = OWNS[to][1:]
             pltpu.make_async_remote_copy(
                 part.at[r, slot * BAND + row : slot * BAND + row + rows],
-                from_a.at[MEMBERS[b].index(dd) * 2 + 1 - r, :rows],
+                from_a.at[own, MEMBERS[b].index(dd) * 2 + xr, :rows],
                 a_send,
-                a_recv,
-                device_id=at(y, 1 - r, to),
+                a_recv.at[own],
+                device_id=at(y, xr, to),
                 device_id_type=MESH,
             ).start()
 
@@ -201,17 +218,21 @@
         c.wait()
     loads[7].wait()
     forward(0)
-    pl.semaphore_wait(bar, jnp.where((d == 0) | (d == 7), 4, jnp.where((d == 3) | (d == 4), 8, 7)))
-    each(range(RING), lambda dd: a_send_half(dd, 0, first_block(dd)))
+    expected = greetings(0)
+    for dd in range(1, RING):
+        expected = jnp.where(d == dd, greetings(dd), expected)
+    pl.semaphore_wait(bar, expected)
 
     @pl.when((d == 3) | (d == 4))
     def _():
         signal(up_sem, at(y, 0, jnp.where(d == 3, 2, 5)))
 
-    @pl.when((d != 0) & (d != 7))
-    def _():
-        for k in (2, ny - 2):
-            signal(ring_sem, at(ring(k), 0, d))
+    def a_start(dd):
+        a_send_half(dd, 0, first_block(dd))
+        for k in (2, ny - 2) if OWNS[dd] else ():
+            signal(ring_sem, at(ring(k), 0, dd))
+
+    each(range(RING), a_start)
 
     for c in loads[4:7]:
         c.wait()
@@ -230,28 +251,22 @@
     load(rowi_in.at[d], rowi)
     load(mom_in, mom)
 
-    def b_copies(dd, src, dst, send, recv):
-        b, row, rows = OWNS[dd]
-        count = 0
-        for m in MEMBERS[b]:
+    def b_copies(dd, b, src, dst, send, recv):
+        own, row, rows = share(dd, b)
+        for m, xr in partners(dd, b, (1, 0)):
             slot = blocks_of(m).index(b)
-            for xr in (1, 0):
-                if (m, xr) != (dd, 0):
-                    count += 1
-                    pltpu.make_async_remote_copy(
-                        src(xr),
-                        dst(xr, slice(slot * BAND + row, slot * BAND + row + rows)),
-                        send,
-                        recv.at[slot],
-                        device_id=at(y, xr, m),
-                        device_id_type=MESH,
-                    ).start()
-        return count
-
-    def own_rows(dd):
-        b, row, rows = OWNS[dd]
-        start = blocks_of(dd).index(b) * BAND + row
-        return slice(start, start + rows)
+            pltpu.make_async_remote_copy(
+                src(own, xr, rows),
+                dst(xr, slice(slot * BAND + row, slot * BAND + row + rows)),
+                send,
+                recv.at[slot],
+                device_id=at(y, xr, m),
+                device_id_type=MESH,
+            ).start()
+
+    def own_rows(dd, b):
+        start = blocks_of(dd).index(b) * BAND + share(dd, b)[1]
+        return slice(start, start + share(dd, b)[2])
 
     def band_part(xr, at_rows):
         return band.at[1 - xr, at_rows]
@@ -260,31 +275,33 @@
         return total.at[at_rows, half_cols()]
 
     def gather_a(dd):
-        b, row, rows = OWNS[dd]
-        wait_rows(None, a_recv, rows, 2 * len(MEMBERS[b]) - 1)
-        mine, other = part[1, own_rows(dd)], None
-        for n, m in enumerate(MEMBERS[b]):
-            if m != dd:
-                mine = mine + from_a[2 * n, :rows]
-            got = from_a[2 * n + 1, :rows]
-            other = got if other is None else other + got
-        from_y[y, :rows] = mine + other
-        sums[0, :rows] = mine
-        sums[1, :rows] = other
-        pl.semaphore_wait(ring_sem, 2)
-        for k in (4, 3, 5, 2, 6, 1, 7):
-            pltpu.make_async_remote_copy(
-                from_y.at[y, :rows], from_y.at[y, :rows], y_send, y_recv, device_id=at(ring(k), 0, dd), device_id_type=MESH
-            ).start()
-        b_copies(dd, lambda xr: sums.at[xr, :rows], band_part, b_send, b_recv)
-        band[1, own_rows(dd)] = mine
-
-    each(OWNS, gather_a)
+        for n, (b, row, rows) in enumerate(OWNS[dd]):
+            wait_rows(None, a_recv.at[n], rows, 2 * len(MEMBERS[b]) - 1)
+            mine, other = part[1, own_rows(dd, b)], None
+            for k, m in enumerate(MEMBERS[b]):
+                if m != dd:
+                    mine = mine + from_a[n, 2 * k, :rows]
+                got = from_a[n, 2 * k + 1, :rows]
+                other = got if other is None else other + got
+            from_y[n, y, :rows] = mine + other
+            sums[n, 0, :rows] = mine
+            sums[n, 1, :rows] = other
+            if n == 0:
+                pl.semaphore_wait(ring_sem, 2)
+            for k in (4, 3, 5, 2, 6, 1, 7):
+                pltpu.make_async_remote_copy(
+                    from_y.at[n, y, :rows], from_y.at[n, y, :rows], y_send.at[n], y_recv.at[n],
+                    device_id=at(ring(k), 0, dd), device_id_type=MESH,
+                ).start()
+            b_copies(dd, b, lambda own, xr, rows: sums.at[own, xr, :rows], band_part, b_send, b_recv)
+            band[1, own_rows(dd, b)] = mine
+
+    each(range(RING), gather_a)
 
     def b_wait(recv):
         def go(dd):
             for slot, b in enumerate(blocks_of(dd)):
-                wait_rows(None, recv.at[slot], 2 * BAND - (OWNS[dd][2] if dd in owners_of(b) else 0))
+                wait_rows(None, recv.at[slot], 2 * BAND - share(dd, b)[2])
 
         each(range(RING), go)
 
@@ -297,28 +314,23 @@
         res[r, :, at_c] = res[r, :, at_c] - sent[ROWS_DEV * c : ROWS_DEV * (c + 1)]
 
     def gather_y(dd):
-        b, row, rows = OWNS[dd]
-        wait_rows(None, y_recv, rows, ny - 1)
-        whole = from_y[0, :rows]
-        for n in range(1, ny):
-            whole = whole + from_y[n, :rows]
-        whole = whole * (1.0 / (2 * ny))
-        sums[2, :rows] = whole
-        b_copies(dd, lambda xr: sums.at[2, :rows], total_part, t_send, t_recv)
-        total[own_rows(dd), half_cols()] = whole
-        wait_rows(y_send, None, rows, ny - 1)
-        for sem in (b_send, t_send):
-            wait_rows(sem, None, rows, 2 * len(MEMBERS[b]) - 1)
-
-    each(OWNS, gather_y)
-
-    def a_sent(dd):
-        rows = 2 * BAND - (OWNS[dd][2] if dd in OWNS else 0)
-        wait_rows(a_send, None, rows)
-        if dd in (2, 5):
-            wait_rows(a_send, None, 2 * BAND)
-
-    each(range(RING), a_sent)
+        for n, (b, row, rows) in enumerate(OWNS[dd]):
+            wait_rows(None, y_recv.at[n], rows, ny - 1)
+            whole = from_y[n, 0, :rows]
+            for k in range(1, ny):
+                whole = whole + from_y[n, k, :rows]
+            whole = whole * (1.0 / (2 * ny))
+            sums[n, 2, :rows] = whole
+            b_copies(dd, b, lambda own, xr, rows: sums.at[own, 2, :rows], total_part, t_send, t_recv)
+            total[own_rows(dd, b), half_cols()] = whole
+        for b in blocks_of(dd):
+            wait_rows(a_send, None, 2 * BAND - share(dd, b)[2])
+        for n, (b, row, rows) in enumerate(OWNS[dd]):
+            wait_rows(y_send.at[n], None, rows, ny - 1)
+            for sem in (b_send, t_send):
+                wait_rows(sem, None, rows, 2 * len(MEMBERS[b]) - 1)
+
+    each(range(RING), gather_y)
     b_wait(t_recv)
 
 
@@ -395,12 +407,12 @@
                 pltpu.VMEM(col_fwd.shape, bf16),
                 pltpu.VMEM(row_fwd.shape[1:], bf16),
                 pltpu.VMEM((2, 2 * BAND, hc), f32),
-                pltpu.VMEM((8, MOST, hc), f32),
-                pltpu.VMEM((3, MOST, hc), f32),
-                pltpu.VMEM((ny, MOST, hc), f32),
+                pltpu.VMEM((2, 8, MOST, hc), f32),
+                pltpu.VMEM((2, 3, MOST, hc), f32),
+                pltpu.VMEM((2, ny, MOST, hc), f32),
                 pltpu.VMEM((2, 2 * BAND, hc), f32),
                 dma((11,)), regular, regular,
-                dma, dma, dma, dma, dma, dma((2,)), dma, dma((2,)),
+                dma, dma((2,)), dma((2,)), dma((2,)), dma, dma((2,)), dma, dma((2,)),
             ],
             compiler_params=pltpu.CompilerParams(
                 collective_id=0, has_side_effects=True, vmem_limit_bytes=24 * 1024 * 1024

time: 22.9 us -> 22.1 us (0.965)
  the two profiles are of different devices: /device:TPU:65 before, /device:TPU:1 now
where the time goes in v5:
time: 22.1 us; the launch traced here: 21.8 us
  Pallas kernels  21.1 us (95%)
  between operations  0.64 us (3%)
    pallas_call x1, Pallas kernels, per_device(): pl.pallas_call(functools.partial(kernel, ny, cols), name='exchange', out_...  19.7 us
    pallas_call x1, Pallas kernels, per_device(): pl.pallas_call(functools.partial(finish, cols), name='finish', out_shape=...  1.44 us

profile of v5, /device:TPU:1, one launch (start us, length us, event | category | flops | bytes accessed | tf_op | source)
XLA Modules:
  0.0 21.8 jit_solution(14840321917864643900)
XLA Ops:
  0.6 19.7 %exchange.1 = (f32[64,768]{1,0:T(8,128)S(1)}, f32[2,48,1536]{2,1,0:T(8,128)S(1)}, f32[2,48,1536]{2,1,0:T(8,128)S(1)}, f32[48,3072]{1,0:T(8,128)S(1)}, bf16[384,5...) custom-call(bf16[1,48,3072]{2,1,0:T(8,128)(2,1)} %inner_in.1, f32[48,3072]{1,0:T(8,128)} %outer_in.1, f32[48,3072]{1,0:T(8,128)} %mom_in.1, ...), custom_call_target="tpu_custom_call" | custom-call | tf_op jit(solution)/shard_map/exchange/pallas_call | solution.py:392
  20.3 1.4 %finish.1 = (f32[48,3072]{1,0:T(8,128)}, f32[48,3072]{1,0:T(8,128)}, f32[1,48,3072]{2,1,0:T(8,128)}) custom-call(f32[64,768]{1,0:T(8,128)S(1)} %get-tuple-element.9.total, f32[2,48,1536]{2,1,0:T(8,128)S(1)} %get-tuple-element.10.res, f32[2,48,1536]{2,1,0:T(8,128)S(1)} %get-tuple-element.11.outer, f32[48,3072]{1,0:T(8,128)S(1)} %get-tuple-element.12.mom, ...), custom_call_target="tpu_custom_call" | custom-call | tf_op jit(solution)/shard_map/finish/pallas_call | solution.py:422

commit v6 on v5

--- a/solution.py
+++ b/solution.py
@@ -79,7 +79,7 @@
 
 
 OWNS = (
-    [], [(0, 0, 24)], [(0, 24, 8), (1, 0, 8)], [(1, 8, 8)], [(1, 16, 8)], [(1, 24, 8), (2, 0, 8)], [(2, 8, 24)], [],
+    [], [(0, 0, 24)], [(0, 24, 8), (1, 0, 8)], [(1, 8, 8)], [(1, 16, 8)], [(1, 24, 8), (2, 0, 8)], [(2, 8, 16)], [(2, 24, 8)],
 )
 MEMBERS = ((0, 1, 2), (2, 3, 4, 5), (5, 6, 7))
 MOST = 24

time: 22.1 us -> 21.9 us (level)
  no operation moved by 1% of the time
where the time goes in v6:
time: 21.9 us; the launch traced here: 21.7 us
  Pallas kernels  21.1 us (96%)
  between operations  0.64 us (3%)
    pallas_call x1, Pallas kernels, per_device(): pl.pallas_call(functools.partial(kernel, ny, cols), name='exchange', out_...  19.6 us
    pallas_call x1, Pallas kernels, per_device(): pl.pallas_call(functools.partial(finish, cols), name='finish', out_shape=...  1.44 us

profile of v6, /device:TPU:1, one launch (start us, length us, event | category | flops | bytes accessed | tf_op | source)
XLA Modules:
  0.0 21.7 jit_solution(11668102923608340861)
XLA Ops:
  0.6 19.6 %exchange.1 = (f32[64,768]{1,0:T(8,128)S(1)}, f32[2,48,1536]{2,1,0:T(8,128)S(1)}, f32[2,48,1536]{2,1,0:T(8,128)S(1)}, f32[48,3072]{1,0:T(8,128)S(1)}, bf16[384,5...) custom-call(bf16[1,48,3072]{2,1,0:T(8,128)(2,1)} %inner_in.1, f32[48,3072]{1,0:T(8,128)} %outer_in.1, f32[48,3072]{1,0:T(8,128)} %mom_in.1, ...), custom_call_target="tpu_custom_call" | custom-call | tf_op jit(solution)/shard_map/exchange/pallas_call | solution.py:392
  20.3 1.4 %finish.1 = (f32[48,3072]{1,0:T(8,128)}, f32[48,3072]{1,0:T(8,128)}, f32[1,48,3072]{2,1,0:T(8,128)}) custom-call(f32[64,768]{1,0:T(8,128)S(1)} %get-tuple-element.9.total, f32[2,48,1536]{2,1,0:T(8,128)S(1)} %get-tuple-element.10.res, f32[2,48,1536]{2,1,0:T(8,128)S(1)} %get-tuple-element.11.outer, f32[48,3072]{1,0:T(8,128)S(1)} %get-tuple-element.12.mom, ...), custom_call_target="tpu_custom_call" | custom-call | tf_op jit(solution)/shard_map/finish/pallas_call | solution.py:422

commit v7 on v6

--- a/solution.py
+++ b/solution.py
@@ -156,13 +156,15 @@
     bar = pltpu.get_barrier_semaphore()
 
     def greet(dd):
-        for b in blocks_of(dd):
-            for m, xr in partners(dd, b, (1, 0)):
-                if greets(dd, b, m):
+        near = [
+            (abs(m // 2 - dd // 2) + xr, m, xr) for b in blocks_of(dd) for m, xr in partners(dd, b, (1, 0)) if greets(dd, b, m)
+        ]
+        for far in (True, False):
+            for k in ((2, ny - 2) if far else (1, ny - 1)) if OWNS[dd] else ():
+                signal(bar, at(ring(k), 0, dd))
+            for hops, m, xr in near:
+                if (hops > 1) == far:
                     signal(bar, at(y, xr, m))
-
-        for k in (2, ny - 2, 1, ny - 1) if OWNS[dd] else ():
-            signal(bar, at(ring(k), 0, dd))
 
     each(range(RING), greet)
 
@@ -178,14 +180,19 @@
 
     chunks = wide // 512
 
-    def forward(r):
-        acc = outer[r] - inner[r].astype(jnp.float32) + res[r]
-        res[r] = acc
-        hi, lo = split(jnp.concatenate([acc[:, 512 * c : 512 * (c + 1)] for c in range(chunks)], axis=0))
+    def forward():
+        pieces = []
+        for r in range(2):
+            acc = outer[r] - inner[r].astype(jnp.float32) + res[r]
+            res[r] = acc
+            pieces += [acc[:, 512 * c : 512 * (c + 1)] for c in range(chunks)]
+        hi, lo = split(jnp.concatenate(pieces, axis=0))
         prod = dot(hi, colf[...])
         tall = prod[:, :128] + prod[:, 128:] + dot(lo, colf[:, :128])
-        hi, lo = split(jnp.concatenate([tall[ROWS_DEV * c : ROWS_DEV * (c + 1)] for c in range(chunks)], axis=1))
-        part[r] = dot(rowf[...], jnp.concatenate([hi, lo, hi], axis=0))
+        hi, lo = split(jnp.concatenate([tall[ROWS_DEV * c : ROWS_DEV * (c + 1)] for c in range(2 * chunks)], axis=1))
+        whole = dot(rowf[...], jnp.concatenate([hi, lo, hi], axis=0))
+        part[0] = whole[:, :hc]
+        part[1] = whole[:, hc:]
 
     def half_cols():
         return pl.ds(pl.multiple_of(xl * hc, 128), hc)
@@ -217,7 +224,9 @@
     for c in loads[:4]:
         c.wait()
     loads[7].wait()
-    forward(0)
+    for c in loads[4:7]:
+        c.wait()
+    forward()
     expected = greetings(0)
     for dd in range(1, RING):
         expected = jnp.where(d == dd, greetings(dd), expected)
@@ -228,24 +237,20 @@
         signal(up_sem, at(y, 0, jnp.where(d == 3, 2, 5)))
 
     def a_start(dd):
-        a_send_half(dd, 0, first_block(dd))
+        for r in range(2):
+            a_send_half(dd, r, first_block(dd))
         for k in (2, ny - 2) if OWNS[dd] else ():
             signal(ring_sem, at(ring(k), 0, dd))
 
     each(range(RING), a_start)
 
-    for c in loads[4:7]:
-        c.wait()
-    forward(1)
 
     def a_rest(dd):
-        a_send_half(dd, 1, first_block(dd))
-        if dd in (2, 5):
-            pl.semaphore_wait(up_sem, 1)
-            for r in range(2):
-                a_send_half(dd, r, 1)
-
-    each(range(RING), a_rest)
+        pl.semaphore_wait(up_sem, 1)
+        for r in range(2):
+            a_send_half(dd, r, 1)
+
+    each((2, 5), a_rest)
 
     load(coli_in, coli)
     load(rowi_in.at[d], rowi)

time: 21.9 us -> 21.8 us (level)
  no operation moved by 1% of the time
where the time goes in v7:
time: 21.8 us; the launch traced here: 21.7 us
  Pallas kernels  21 us (96%)
  between operations  0.64 us (3%)
    pallas_call x1, Pallas kernels, per_device(): pl.pallas_call(functools.partial(kernel, ny, cols), name='exchange', out_...  19.6 us
    pallas_call x1, Pallas kernels, per_device(): pl.pallas_call(functools.partial(finish, cols), name='finish', out_shape=...  1.43 us

profile of v7, /device:TPU:1, one launch (start us, length us, event | category | flops | bytes accessed | tf_op | source)
XLA Modules:
  0.0 21.7 jit_solution(11487803194050840913)
XLA Ops:
  0.6 19.6 %exchange.1 = (f32[64,768]{1,0:T(8,128)S(1)}, f32[2,48,1536]{2,1,0:T(8,128)S(1)}, f32[2,48,1536]{2,1,0:T(8,128)S(1)}, f32[48,3072]{1,0:T(8,128)S(1)}, bf16[384,5...) custom-call(bf16[1,48,3072]{2,1,0:T(8,128)(2,1)} %inner_in.1, f32[48,3072]{1,0:T(8,128)} %outer_in.1, f32[48,3072]{1,0:T(8,128)} %mom_in.1, ...), custom_call_target="tpu_custom_call" | custom-call | tf_op jit(solution)/shard_map/exchange/pallas_call | solution.py:397
  20.2 1.4 %finish.1 = (f32[48,3072]{1,0:T(8,128)}, f32[48,3072]{1,0:T(8,128)}, f32[1,48,3072]{2,1,0:T(8,128)}) custom-call(f32[64,768]{1,0:T(8,128)S(1)} %get-tuple-element.9.total, f32[2,48,1536]{2,1,0:T(8,128)S(1)} %get-tuple-element.10.res, f32[2,48,1536]{2,1,0:T(8,128)S(1)} %get-tuple-element.11.outer, f32[48,3072]{1,0:T(8,128)S(1)} %get-tuple-element.12.mom, ...), custom_call_target="tpu_custom_call" | custom-call | tf_op jit(solution)/shard_map/finish/pallas_call | solution.py:427
